TPU v7x, 256 devices: a whole 4x4x8 slice. The times are simulated.
256 devices in a mesh: dp: 16 (over y, x), tensor: 16 (over z, core).
Axes of the slice: x: 4, y: 4, z: 8, core: 2. Of those that a mesh axis runs over, the one named last changes fastest.
Arguments:
- hidden_in: bfloat16 [32768, 8192], P('dp', 'tensor'), may hold values from -6 to 6
- grad_gate: bfloat16 [32768, 16384], P('dp', 'tensor'), may hold values from -6 to 6
- adapter_in: bfloat16 [64, 16, 8192], P('dp', None, 'tensor'), may hold values from -0.23925781 to 0.23925781
- adapter_out: bfloat16 [64, 16, 16384], P('dp', None, 'tensor'), may hold values from -0.046875 to 0.046875
- block_tenant: int32 [256], replicated, may hold values from 0 to 63
- block_dest: int32 [256, 1], replicated, may hold values from 0 to 15; in each aligned block of 16 rows (0 to 15, 16 to 31, ...) at most 2 rows name the same one
- tenant_tokens: int32 [64], replicated, may hold values from 128 to 1024
- tenant_owner: int32 [64], replicated, may hold values from 0 to 63, each once
Outputs:
- dgrad_placed: bfloat16 [65536, 8192], P('dp', 'tensor')
- grad_in: float32 [64, 16, 8192], P('dp', None, 'tensor')
- grad_out: float32 [64, 16, 16384], P('dp', None, 'tensor')
- tenant_norms: float32 [64], P('dp')
Inputs may be any that keep to these rules, and one draw needn't show every extreme that they name: `block_dest`: among the 16 blocks of one data group (blocks g * 16 to g * 16 + 15) at most 2 name the same destination group, and in some data group exactly 2 name one destination. `tenant_owner`: A permutation: every row of 0 to 63 belongs to exactly one tenant.
All inputs are finite; a program needn't handle non-finite values.
Results may differ from a plain program's by a relative error of at most 0.0049.
Values may be sent and summed in bfloat16 or wider, within the bound.
A program may use at most 128 MiB of HBM per device.

v0:
```python
import jax
import jax.numpy as jnp
from jax import lax
from jax.sharding import PartitionSpec as P

ADAPTER_RANK = 16
PLAN_BLOCK_ROWS = 128


adapter_scale = 2.0


def choose_rows(lookup, indices):
    entries = lookup.shape[0]
    select = (indices[:, None] == jnp.arange(entries, dtype=jnp.int32)[None, :]).astype(
        jnp.bfloat16
    )
    flat_table = lookup.reshape(entries, -1)
    picked = jnp.dot(select, flat_table, preferred_element_type=jnp.float32).astype(jnp.bfloat16)
    return picked.reshape((indices.shape[0],) + lookup.shape[1:])


def group_terms(partials, indices, is_live, entries):
    select = (
        (indices[None, :] == jnp.arange(entries, dtype=jnp.int32)[:, None]) & is_live[None, :]
    ).astype(jnp.float32)
    flat_terms = partials.reshape(partials.shape[0], -1)
    summed = jnp.dot(
        select, flat_terms, precision=lax.Precision.HIGHEST, preferred_element_type=jnp.float32
    )
    return summed.reshape((entries,) + partials.shape[1:])


def rank_factors(rows_x, gradient_rows, mat_in, output_matrix):
    local_blocks = rows_x.shape[0]
    low_part = jnp.einsum(
        "nbc,nrc->nbr", rows_x, mat_in, preferred_element_type=jnp.float32
    ).reshape(local_blocks, -1)
    back_part = jnp.einsum(
        "nbf,nrf->nbr", gradient_rows, output_matrix, preferred_element_type=jnp.float32
    ).reshape(local_blocks, -1)
    low_sum, backward_total = lax.psum((low_part, back_part), "tensor")
    rank_product = low_sum.reshape(local_blocks, PLAN_BLOCK_ROWS, ADAPTER_RANK).astype(jnp.bfloat16)
    rank_matrix = (
        (adapter_scale * backward_total)
        .reshape(local_blocks, PLAN_BLOCK_ROWS, ADAPTER_RANK)
        .astype(jnp.bfloat16)
    )
    return (rank_product, rank_matrix)


def block_grads(rows_x, gradient_rows, rank_product, rank_matrix, weight_matrices):
    part_in = (
        jnp.einsum("nbr,nbc->nrc", rank_matrix, rows_x, preferred_element_type=jnp.float32)
        * weight_matrices[:, None, None]
    )
    partial_output = (
        jnp.einsum("nbr,nbf->nrf", rank_product, gradient_rows, preferred_element_type=jnp.float32)
        * (adapter_scale * weight_matrices)[:, None, None]
    )
    return (part_in, partial_output)


def place_blocks(blocks, places, slot_count):
    empty = jnp.zeros((slot_count,) + blocks.shape[1:], blocks.dtype)
    return empty.at[places].set(blocks)


def apply_factor(rank_matrix, mat_in):
    return jnp.einsum(
        "nbr,nrc->nbc", rank_matrix, mat_in, preferred_element_type=jnp.float32
    ).astype(jnp.bfloat16)


def per_device(
    hidden_in,
    grad_gate,
    adapter_in,
    adapter_out,
    block_tenant,
    block_dest,
    tenant_tokens,
    tenant_owner,
):
    groups = lax.axis_size("dp")
    my_group = lax.axis_index("dp")
    all_blocks = block_tenant.shape[0]
    group_blocks = all_blocks // groups
    per_pair = max(2, 2 * group_blocks // groups)
    slot_count = groups * per_pair
    cols_d = hidden_in.shape[1]
    cols_f = grad_gate.shape[1]
    all_in, all_out = (
        lax.all_gather(adapter_in, "dp", axis=0, tiled=True),
        lax.all_gather(adapter_out, "dp", axis=0, tiled=True),
    )
    ten_all = all_in.shape[0]
    position = tenant_owner[block_tenant]
    weight_matrices = 1.0 / tenant_tokens[block_tenant].astype(jnp.float32)
    target = block_dest[:, 0]
    matches = (target[:, None] == jnp.arange(groups, dtype=jnp.int32)[None, :]).astype(jnp.int32)
    matches = matches.reshape(groups, group_blocks, groups)
    within = jnp.sum((jnp.cumsum(matches, axis=1) - matches) * matches, axis=2).reshape(all_blocks)
    source = jnp.arange(all_blocks, dtype=jnp.int32) // group_blocks
    to_here = target == my_group
    arrive = jnp.where(to_here, source * per_pair + within, slot_count)
    slot_pos = jnp.zeros((slot_count,), jnp.int32).at[arrive].set(position, mode="drop")
    slot_weight = jnp.ones((slot_count,), jnp.float32).at[arrive].set(weight_matrices, mode="drop")
    slot_live = jnp.zeros((slot_count,), jnp.bool_).at[arrive].set(True, mode="drop")
    first_block = my_group * group_blocks
    own_slot = lax.dynamic_slice_in_dim(target * per_pair + within, first_block, group_blocks)
    rows_x = hidden_in.reshape(group_blocks, PLAN_BLOCK_ROWS, cols_d)
    gradient_rows = grad_gate.reshape(group_blocks, PLAN_BLOCK_ROWS, cols_f)
    send_x = place_blocks(rows_x, own_slot, slot_count).reshape(
        slot_count * PLAN_BLOCK_ROWS, cols_d
    )
    send_g = place_blocks(gradient_rows, own_slot, slot_count).reshape(
        slot_count * PLAN_BLOCK_ROWS, cols_f
    )
    got_x, got_g = (
        lax.all_to_all(send_x, "dp", split_axis=0, concat_axis=0, tiled=True),
        lax.all_to_all(send_g, "dp", split_axis=0, concat_axis=0, tiled=True),
    )
    got_x = got_x.reshape(slot_count, PLAN_BLOCK_ROWS, cols_d)
    got_g = got_g.reshape(slot_count, PLAN_BLOCK_ROWS, cols_f)
    mat_in = choose_rows(all_in, slot_pos)
    output_matrix = choose_rows(all_out, slot_pos)
    rank_product, rank_matrix = rank_factors(got_x, got_g, mat_in, output_matrix)
    dgrad_rows = apply_factor(rank_matrix, mat_in)
    part_in, partial_output = block_grads(got_x, got_g, rank_product, rank_matrix, slot_weight)
    term_in = group_terms(part_in, slot_pos, slot_live, ten_all)
    term_out = group_terms(partial_output, slot_pos, slot_live, ten_all)
    grad_in, grad_out = (
        lax.psum_scatter(term_in, "dp", scatter_dimension=0, tiled=True),
        lax.psum_scatter(term_out, "dp", scatter_dimension=0, tiled=True),
    )
    squares = jnp.sum(grad_in * grad_in, axis=(1, 2)) + jnp.sum(grad_out * grad_out, axis=(1, 2))
    squares_all = lax.psum(squares, "tensor")
    return (
        dgrad_rows.reshape(slot_count * PLAN_BLOCK_ROWS, cols_d),
        grad_in,
        grad_out,
        jnp.sqrt(squares_all),
    )


def solution(mesh):
    return jax.shard_map(
        per_device,
        mesh=mesh,
        in_specs=(
            P("dp", "tensor"),
            P("dp", "tensor"),
            P("dp", None, "tensor"),
            P("dp", None, "tensor"),
            P(),
            P(),
            P(),
            P(),
        ),
        out_specs=(P("dp", "tensor"), P("dp", None, "tensor"), P("dp", None, "tensor"), P("dp")),
        check_vma=False,
    )
```

profile of v0, /device:TPU:1, one launch (start us, length us, event | category | flops | bytes accessed | tf_op | source)
XLA Modules:
  0.0 558.2 jit_solution(1823301160828340478)
XLA Ops:
  7.2 0.5 broadcast.105
  7.7 1.3 reduce.3
  9.2 0.5 fusion.27
  9.7 0.1 reshape.136
  9.9 0.7 compare_select_fusion
  10.7 4.3 broadcast_in_dim.20
  15.0 10.9 %scatter_fusion = bf16[32,128,1024]{2,1,0:T(8,128)(2,1)} fusion(bf16[32,128,1024]{2,1,0:T(8,128)(2,1)} %broadcast_in_dim.20, s32[16]{0:T(128)S(1)} %compare_select_fusion.3, bf16[16,128,1024]{2,1,0:T(8,128)(2,1)} %bitcast.70), kind=kCustom, calls=%fused_computation.2 | custom fusion | bytes 12582976 | tf_op jit(solution)/shard_map/scatter | solution.py:66
  25.9 7.7 %all-to-all-start = ((bf16[16,256,1024]{2,1,0:T(8,128)(2,1)}), bf16[16,256,1024]{2,1,0:T(8,128)(2,1)}, u32[]{:S(2)}, u32[]{:S(2)}) async-start(bf16[16,256,1024]{2,1,0:T(8,128)(2,1)} %bitcast.60), calls=%async_computation | async-start | bytes 16777216 | tf_op jit(solution)/shard_map/all_to_all | solution.py:122
  33.7 0.7 all-gather.3.cloned.1.call-update
  34.4 2.5 broadcast_in_dim.27
  36.8 5.1 scatter_fusion.1
  42.0 119.8 %all-to-all-done = bf16[16,256,1024]{2,1,0:T(8,128)(2,1)} async-done(((bf16[16,256,1024]{2,1,0:T(8,128)(2,1)}), bf16[16,256,1024]{2,1,0:T(8,128)(2,1)}, u32[]{:S(2)}, u32[]{:S(2)}) %all-to-all-start) | async-done | bytes 8388640 | tf_op jit(solution)/shard_map/all_to_all | solution.py:122
  161.8 6.7 %all-to-all-start.1 = ((bf16[16,256,512]{2,1,0:T(8,128)(2,1)}), bf16[16,256,512]{2,1,0:T(8,128)(2,1)}, u32[]{:S(2)}, u32[]{:S(2)}) async-start(bf16[16,256,512]{2,1,0:T(8,128)(2,1)} %bitcast.61), calls=%async_computation.1 | async-start | bytes 8388608 | tf_op jit(solution)/shard_map/all_to_all | solution.py:121
  168.7 1.9 gather_fusion
  170.5 1.4 scatter_custom_fusion.1
  172.0 2.8 copy.49
  174.8 0.5 convolution_convert_fusion
  175.3 0.6 copy.50
  175.9 5.7 %fusion.28 = f32[32,128,16]{1,2,0:T(8,128)S(1)} fusion(bf16[32,128,1024]{2,1,0:T(8,128)(2,1)} %bitcast.3, bf16[32,16,1024]{2,1,0:T(8,128)(2,1)S(1)} %bitcast.66), kind=kOutput, calls=%fused_computation.59 | convolution fusion | flops 134217728 | bytes 9699328 | tf_op jit(solution)/shard_map/nbf,nrf->nbr/dot_general | solution.py:39
  181.5 1.4 copy.38
  183.0 0.7 all-gather.5.cloned.1.call-update
  183.8 1.9 gather_fusion.1
  185.7 1.4 scatter_custom_fusion.4
  187.1 1.7 scatter_custom_fusion.2
  188.8 114.2 %all-reduce.3.cloned.1.call-done = f32[32,2048]{0,1:T(8,128)} async-done(((f32[32,2048]{0,1:T(8,128)}), f32[32,2048]{0,1:T(8,128)}) %all-reduce.3.cloned.1.call-update) | async-done | bytes 262160 | tf_op jit(solution)/shard_map/psum | solution.py:42
  302.9 1.3 multiply_convert_fusion
  304.2 0.5 copy.39
  304.7 2.8 convolution_multiply_fusion.1
  307.6 1.7 fusion.4
  309.3 2.6 copy.42
  312.0 40.4 %all-gather.5.cloned.1.call-done = bf16[64,16,512]{2,1,0:T(8,128)(2,1)} async-done(((bf16[4,16,512]{2,1,0:T(8,128)(2,1)}), bf16[64,16,512]{2,1,0:T(8,128)(2,1)}) %all-gather.5.cloned.1.call-update) | async-done | bytes 1048592 | tf_op jit(solution)/shard_map/all_gather | solution.py:94
  352.4 1.8 copy.51
  354.2 0.4 convolution_convert_fusion.1
  354.6 0.2 copy.52
  354.7 3.4 fusion.29
  358.1 0.6 copy.43
  358.7 57.3 %all-reduce.4 = bf16[32,2048]{0,1:T(8,128)(2,1)S(1)} all-reduce(f32[32,2048]{0,1:T(8,128)S(1)} %bitcast.67), channel_id=1, replica_groups=mesh['dp'=16,'tensor'=16] {'tensor'}, use_global_device_ids=true, to_apply=%region_9.10 | all-reduce | flops 65536 | bytes 393216 | tf_op jit(solution)/shard_map/psum | solution.py:42
  416.0 0.5 copy.44
  416.5 4.6 convolution_multiply_fusion
  421.1 3.3 fusion
  424.4 4.4 copy.46
  428.9 6.2 %reduce-scatter.3.cloned.1.call-done = f32[4,16,512]{2,1,0:T(8,128)} async-done(((f32[64,16,512]{2,1,0:T(8,128)}), f32[4,16,512]{2,1,0:T(8,128)}) %reduce-scatter.3.cloned.1.call-update) | async-done | bytes 131088 | tf_op jit(solution)/shard_map/reduce_scatter | solution.py:134
  435.1 1.0 multiply_reduce_fusion.1
  436.1 85.0 %reduce-scatter.5.cloned.1.call-done = f32[4,16,1024]{2,1,0:T(8,128)} async-done(((f32[64,16,1024]{2,1,0:T(8,128)}), f32[4,16,1024]{2,1,0:T(8,128)}) %reduce-scatter.5.cloned.1.call-update) | async-done | bytes 262160 | tf_op jit(solution)/shard_map/reduce_scatter | solution.py:135
  521.1 1.1 multiply_reduce_fusion
  522.2 3.3 convolution_convert_fusion.2
  525.5 25.7 %psum.23 = f32[4]{0:T(128)S(1)} all-reduce(f32[4]{0:T(128)S(1)} %add.57), channel_id=1, replica_groups=mesh['dp'=16,'tensor'=16] {'tensor'}, use_global_device_ids=true, to_apply=%region_13.14 | all-reduce | flops 4 | bytes 32 | tf_op jit(solution)/shard_map/psum | solution.py:138
  551.2 0.5 sqrt.3
  (30 shorter events, 0.7 us)
Async XLA Ops:
  7.2 161.5 %copy-start = (s32[64]{0:T(128)S(1)}, s32[64]{0:T(128)}, u32[]{:S(2)}) copy-start(s32[64]{0:T(128)} %param.15) | copy-start | bytes 772
  25.9 135.9 %all-to-all-start = ((bf16[16,256,1024]{2,1,0:T(8,128)(2,1)}), bf16[16,256,1024]{2,1,0:T(8,128)(2,1)}, u32[]{:S(2)}, u32[]{:S(2)}) async-start(bf16[16,256,1024]{2,1,0:T(8,128)(2,1)} %bitcast.60), calls=%async_computation | async-start | bytes 16777216 | tf_op jit(solution)/shard_map/all_to_all | solution.py:122
  33.6 3.2 copy-start.2
  33.6 138.3 %all-gather.3.cloned.1.call-start = ((), (), s32[]{:S(2)}) async-start(), calls=%async_computation.4 | async-start | bytes 2228224 | tf_op jit(solution)/shard_map/all_gather | solution.py:95
  161.8 6.8 %copy-start.3 = (s32[256]{0:T(256)S(1)}, s32[256]{0:T(256)}, u32[]{:S(2)}) copy-start(s32[256]{0:T(256)} %param.12) | copy-start | bytes 3076
  161.8 142.9 %all-to-all-start.1 = ((bf16[16,256,512]{2,1,0:T(8,128)(2,1)}), bf16[16,256,512]{2,1,0:T(8,128)(2,1)}, u32[]{:S(2)}, u32[]{:S(2)}) async-start(bf16[16,256,512]{2,1,0:T(8,128)(2,1)} %bitcast.61), calls=%async_computation.1 | async-start | bytes 8388608 | tf_op jit(solution)/shard_map/all_to_all | solution.py:121
  168.6 134.4 %all-reduce.3.cloned.1.call-start = ((), (), s32[]{:S(2)}) async-start(), calls=%async_computation.5 | async-start | bytes 2097152 | tf_op jit(solution)/shard_map/psum | solution.py:42
  175.8 7.9 %copy-start.1 = (s32[64]{0:T(128)S(1)}, s32[64]{0:T(128)}, u32[]{:S(2)}) copy-start(s32[64]{0:T(128)} %param.14) | copy-start | bytes 772
  183.0 169.4 %all-gather.5.cloned.1.call-start = ((), (), s32[]{:S(2)}) async-start(), calls=%async_computation.6 | async-start | bytes 1114112 | tf_op jit(solution)/shard_map/all_gather | solution.py:94
  183.7 251.3 %reduce-scatter.3.cloned.1.call-start = ((), (), s32[]{:S(2)}) async-start(), calls=%async_computation.7 | async-start | bytes 2228224 | tf_op jit(solution)/shard_map/reduce_scatter | solution.py:134
  311.9 209.2 %reduce-scatter.5.cloned.1.call-start = ((), (), s32[]{:S(2)}) async-start(), calls=%async_computation.8 | async-start | bytes 4456448 | tf_op jit(solution)/shard_map/reduce_scatter | solution.py:135
Sparse Core Ops, SparseCore 0:
  36.9 131.7 all-gather.2
  183.1 119.7 all-reduce.2
  305.7 46.6 all-gather.4
  356.8 78.2 reduce-scatter.2
  439.1 81.9 reduce-scatter.4
where the time goes:
time: 559 us; the launch traced here: 558 us
  waiting for transfers between devices  367 us (66%)
  blocking collectives  83 us (15%)
  local copies, waits for them, and re-layouts  47.9 us (9%)
  matrix products  25.6 us (5%)
  starting transfers between devices  14.6 us (3%)
  between operations  14 us (3%)
  other arithmetic  6.01 us (1%)
    all_to_all x1, waiting for transfers between devices, per_device(): lax.all_to_all(send_g, 'dp', split_axis=0, concat_axis=0, tiled=True)  120 us
    psum x1, waiting for transfers between devices, rank_factors(): low_sum, backward_total = lax.psum((low_part, back_part), 'tensor')  114 us
    reduce_scatter x1, waiting for transfers between devices, per_device(): lax.psum_scatter(term_out, 'dp', scatter_dimension=0, tiled=True)  85 us
    psum x1, blocking collectives, rank_factors(): low_sum, backward_total = lax.psum((low_part, back_part), 'tensor')  57.3 us
    all_gather x1, waiting for transfers between devices, per_device(): lax.all_gather(adapter_in, 'dp', axis=0, tiled=True)  40.4 us
    psum x1, blocking collectives, per_device(): squares_all = lax.psum(squares, 'tensor')  25.7 us
    scatter x2, local copies, waits for them, and re-layouts, place_blocks(): return empty.at[places].set(blocks)  16.1 us
  transfers between devices with their start and end apart: 7, of which 5 were waited for; matrix products, arithmetic and copies ran while one was open for 10% of the time, Pallas kernels for 0%

commit v1 on v0

v1 whole, which is shorter than its diff:
```python
import functools

import jax
import jax.numpy as jnp
from jax import lax
from jax.experimental import pallas as pl
from jax.experimental.pallas import tpu as pltpu
from jax.sharding import PartitionSpec as P

SIDE = 4
R = 16
ROWS = 128
BLK = 16
OWN = 4
GROUPS = SIDE * SIDE
MESH = pl.DeviceIdType.MESH
BF16 = jnp.bfloat16
F32 = jnp.float32


def remote(src, dst, send_sem, recv_sem, device):
    return pltpu.make_async_remote_copy(
        src_ref=src,
        dst_ref=dst,
        send_sem=send_sem,
        recv_sem=recv_sem,
        device_id=device,
        device_id_type=MESH,
    )


class Ring:
    def __init__(self, buf, here, right, left, sends, recvs, src=None):
        self.buf, self.here, self.right, self.left = buf, here, right, left
        half = buf.shape[1] // 2
        before, after = (here + 3) % SIDE, (here + 1) % SIDE
        own = buf.at[here] if src is None else src
        mine = buf.at[here]
        self.own = [
            remote(own, mine, sends.at[0], recvs.at[0], right),
            remote(own, mine, sends.at[1], recvs.at[1], left),
        ]
        low = buf.at[before, pl.ds(0, half)]
        high = buf.at[after, pl.ds(half, half)]
        self.pass_on = [
            remote(low, low, sends.at[2], recvs.at[2], right),
            remote(high, high, sends.at[3], recvs.at[3], left),
        ]

    def start(self):
        for copy in self.own:
            copy.start()

    def forward(self):
        for copy, onward in zip(self.own, self.pass_on):
            copy.wait_recv()
            onward.start()

    def finish(self):
        for copy in self.pass_on:
            copy.wait_recv()

    def drain(self):
        for copy in self.own + self.pass_on:
            copy.wait_send()


def kernel(
    n_tensor,
    tenant_ref,
    dest_ref,
    tokens_ref,
    owner_ref,
    x_hbm,
    g_hbm,
    ain_hbm,
    aout_hbm,
    dg_hbm,
    gin_hbm,
    gout_hbm,
    norm_ref,
    x_v,
    g_v,
    tab_in,
    tab_out,
    low_part,
    fac_part,
    low_got,
    fac_got,
    low_all,
    fac_all,
    term_in,
    term_out,
    pick,
    sum_in,
    sum_out,
    to_in,
    to_out,
    from_in,
    from_out,
    slot_send,
    slots,
    dg_v,
    gin_v,
    gout_v,
    sq_own,
    sq_got,
    pos_own,
    pos_slot,
    ring_s,
    ring_r,
    z_s,
    z_r,
    slot_s,
    slot_r,
    own_s,
    own_r,
    sq_s,
    sq_r,
    loc,
    dg_sem,
):
    me = lax.axis_index("dp")
    t = lax.axis_index("tensor")
    y, x = me // SIDE, me % SIDE
    bt = BLK // n_tensor
    cd, cf = x_v.shape[1], g_v.shape[1]
    hd, hf = cd // 2, cf // 2

    def at_dp(yy, xx):
        return {"dp": yy * SIDE + xx}

    x_right, x_left = at_dp(y, (x + 1) % SIDE), at_dp(y, (x + 3) % SIDE)
    y_right, y_left = at_dp((y + 1) % SIDE, x), at_dp((y + 3) % SIDE, x)
    along_x, along_y = (x, x_right, x_left), (y, y_right, y_left)

    load_x = pltpu.make_async_copy(x_hbm, x_v, loc.at[0])
    load_g = pltpu.make_async_copy(g_hbm, g_v, loc.at[1])
    in_cols = [ain_hbm.at[:, :, pl.ds(h * hd, hd)] for h in range(2)]
    out_cols = [aout_hbm.at[:, :, pl.ds(h * hf, hf)] for h in range(2)]
    places = [(y, x), (x, y)]
    own_tables = []
    for h in range(2):
        own_tables.append(
            pltpu.make_async_copy(in_cols[h], tab_in[h].at[places[h][0], places[h][1]], loc.at[2 + h])
        )
        own_tables.append(
            pltpu.make_async_copy(
                out_cols[h], tab_out[h].at[places[h][0], places[h][1]], loc.at[4 + h]
            )
        )
    for copy in own_tables:
        copy.start()
    load_x.start()
    load_g.start()

    barrier = pltpu.get_barrier_semaphore()

    def greet_dp(k, _):
        pl.semaphore_signal(
            barrier, inc=1, device_id={"dp": (me + k) % GROUPS}, device_id_type=MESH
        )
        return 0

    def greet_tensor(k, _):
        pl.semaphore_signal(
            barrier, inc=1, device_id={"tensor": (t + k) % n_tensor}, device_id_type=MESH
        )
        return 0

    lax.fori_loop(1, GROUPS, greet_dp, 0)
    lax.fori_loop(1, n_tensor, greet_tensor, 0)

    def place_of(block):
        return owner_ref[tenant_ref[block]]

    def own_places(b, _):
        pos_own[b] = place_of(me * BLK + b)
        return 0

    lax.fori_loop(0, BLK, own_places, 0)
    pl.semaphore_wait(barrier, GROUPS - 1 + n_tensor - 1)

    def ring(number, buf, along, src=None):
        return Ring(buf, along[0], along[1], along[2], ring_s.at[number], ring_r.at[number], src)

    first, second = [along_x, along_y], [along_y, along_x]
    in_1 = [ring(h, tab_in[h].at[places[h][0]], first[h], in_cols[h]) for h in range(2)]
    in_2 = [ring(2 + h, tab_in[h], second[h]) for h in range(2)]
    out_1 = [ring(4 + h, tab_out[h].at[places[h][0]], first[h], out_cols[h]) for h in range(2)]
    out_2 = [ring(6 + h, tab_out[h], second[h]) for h in range(2)]
    for r in in_1 + out_1:
        r.start()
    for copy in own_tables:
        copy.wait()
    for r in in_1 + out_1:
        r.forward()
    for r, after in zip(in_1 + out_1, in_2 + out_2):
        r.finish()
        after.start()

    def slot_places(s, _):
        one, two = jnp.int32(-1), jnp.int32(-1)
        for i in range(BLK):
            b = s * BLK + i
            hit = dest_ref[b] == me
            p = place_of(b)
            two = jnp.where(hit & (one >= 0), p, two)
            one = jnp.where(hit & (one < 0), p, one)
        pos_slot[2 * s] = jnp.maximum(one, 0)
        pos_slot[2 * s + 1] = jnp.maximum(two, 0)
        return 0

    lax.fori_loop(0, GROUPS, slot_places, 0)

    def choose(q, _):
        lane = lax.broadcasted_iota(jnp.int32, (8, 128), 1)
        wide = (SIDE * OWN * R, 128)
        row = lax.broadcasted_iota(jnp.int32, wide, 0)
        same = (row & (R - 1)) == (lax.broadcasted_iota(jnp.int32, wide, 1) & (R - 1))
        tall = row >> 4
        g, first_blk = q // 2, (q % 2) * 8
        for h in range(2):
            group = y * SIDE + g if h == 0 else g * SIDE + x
            want = jnp.full((8, 128), -1, jnp.int32)
            for i in range(8):
                p = place_of(group * BLK + first_blk + i)
                if h == 0:
                    local = jnp.where(((p >> 2) & 3) == x, ((p >> 4) << 2) | (p & 3), -1)
                else:
                    local = jnp.where((p >> 4) == y, p & 15, -1)
                want = jnp.where((lane >> 4) == i, local, want)
            hit = (tall == want[0:1]) & same
            pick[h][:, pl.ds(pl.multiple_of(q * 128, 128), 128)] = jnp.where(hit, 1.0, 0.0).astype(BF16)
        return 0

    lax.fori_loop(0, 2 * SIDE, choose, 0)

    def partial_products(table, rows_v, half, part):
        def one(b, _):
            p = pos_own[b]
            rows = rows_v[pl.ds(pl.multiple_of(b * ROWS, ROWS), ROWS), :]
            tab_a = table[0][p >> 4, (p >> 2) & 3, p & 3]
            tab_b = table[1][(p >> 2) & 3, p >> 4, p & 3]
            nt = (((1,), (1,)), ((), ()))
            part[b] = lax.dot_general(
                tab_a, rows[:, :half], nt, preferred_element_type=F32
            ) + lax.dot_general(tab_b, rows[:, half:], nt, preferred_element_type=F32)
            return 0

        lax.fori_loop(0, BLK, one, 0, unroll=2)

    def reduce_copy(part, got, number, k):
        to = (t + k) % n_tensor
        return remote(
            part.at[pl.ds(to * bt, bt)],
            got.at[k],
            z_s.at[number, k],
            z_r.at[number, k],
            {"tensor": to},
        )

    def spread_copy(full, number, k):
        mine = full.at[pl.ds(t * bt, bt)]
        return remote(
            mine, mine, z_s.at[number, k], z_r.at[number, k], {"tensor": (t + k) % n_tensor}
        )

    def over_tensor(do):
        lax.fori_loop(1, n_tensor, lambda k, _: (do(k), 0)[1], 0)

    def send_parts(part, got, number):
        over_tensor(lambda k: reduce_copy(part, got, number, k).start())

    def add_parts(part, got, full, number, scale):
        over_tensor(lambda k: reduce_copy(part, got, number, k).wait_recv())
        total = lax.fori_loop(1, n_tensor, lambda k, acc: acc + got[k], part[pl.ds(t * bt, bt)])
        full[pl.ds(t * bt, bt)] = (scale * total).astype(BF16)
        over_tensor(lambda k: spread_copy(full, number + 1, k).start())

    def take_spread(full, number):
        over_tensor(lambda k: spread_copy(full, number, k).wait_recv())

    def terms(factor, rows_v, half, out):
        for h in range(2):

            def one(b, _):
                rows = rows_v[pl.ds(pl.multiple_of(b * ROWS, ROWS), ROWS), pl.ds(h * half, half)]
                out[h][first[h][0], b] = jnp.dot(
                    factor[b], rows, preferred_element_type=F32
                ).astype(BF16)
                return 0

            lax.fori_loop(0, BLK, one, 0, unroll=2)

    for r in in_2:
        r.forward()
    for r in in_2:
        r.finish()
    load_x.wait()
    partial_products(tab_in, x_v, hd, low_part)
    send_parts(low_part, low_got, 0)
    for r in out_2:
        r.forward()
    add_parts(low_part, low_got, low_all, 0, 1.0)
    load_g.wait()
    take_spread(low_all, 1)
    term_out_1 = [ring(8 + h, term_out[h], first[h]) for h in range(2)]
    terms(low_all, g_v, hf, term_out)
    for r in term_out_1:
        r.start()
    for r in out_2:
        r.finish()
    partial_products(tab_out, g_v, hf, fac_part)
    send_parts(fac_part, fac_got, 2)
    for r in term_out_1:
        r.forward()
    add_parts(fac_part, fac_got, fac_all, 2, 2.0)
    take_spread(fac_all, 3)
    term_in_1 = [ring(10 + h, term_in[h], first[h]) for h in range(2)]
    terms(fac_all, x_v, hd, term_in)
    for r in term_in_1:
        r.start()

    def slot_copy(k):
        to = (me + k) % GROUPS
        return remote(slot_send.at[k], slots.at[me], slot_s.at[k], slot_r.at[k], {"dp": to})

    def blocks_for(group):
        one, two = jnp.int32(-1), jnp.int32(-1)
        for i in range(BLK):
            hit = dest_ref[me * BLK + i] == group
            two = jnp.where(hit & (one >= 0), i, two)
            one = jnp.where(hit & (one < 0), i, one)
        return one, two

    def masked(i):
        live = jnp.where(i >= 0, 1.0, 0.0).astype(F32)
        return (fac_all[jnp.maximum(i, 0)].astype(F32) * live).astype(BF16)

    def pack(k, _):
        one, two = blocks_for((me + k) % GROUPS)
        slot_send[k, 0] = masked(one)
        slot_send[k, 1] = masked(two)
        slot_copy(k).start()
        return 0

    lax.fori_loop(1, GROUPS, pack, 0)
    one, two = blocks_for(me)
    slots[me, 0] = masked(one)
    slots[me, 1] = masked(two)

    def owner_copies(number, h, sends, lands):
        here = second[h][0]
        copies = []
        for k in range(1, SIDE):
            to = (here + k) % SIDE
            device = at_dp(to, x) if h == 0 else at_dp(y, to)
            copies.append(
                remote(
                    sends.at[to],
                    lands.at[k - 1],
                    own_s.at[number, k - 1],
                    own_r.at[number, k - 1],
                    device,
                )
            )
        return copies

    def add_terms(h, term, total, sends):
        cols = total.shape[1]
        step = min(cols, 256)
        rows = SIDE * OWN * R

        def one(c, _):
            where = pl.ds(pl.multiple_of(c * step, step), step)
            block = term[:, :, :, where].reshape(SIDE * BLK * R, step)
            out = jnp.dot(pick[h][...], block, preferred_element_type=F32)
            total[:, where] = out
            sends[:, :, where] = out.reshape(SIDE, OWN * R, step).astype(BF16)
            return 0

        lax.fori_loop(0, cols // step, one, 0)

    def own_sum(h, total, lands, result, scale, half):
        here = second[h][0]
        kept = total[pl.ds(pl.multiple_of(here * OWN * R, OWN * R), OWN * R), :]
        for k in range(SIDE - 1):
            kept = kept + lands[k].astype(F32)
        squares = []
        for j in range(OWN):
            piece = kept[j * R : (j + 1) * R] * scale[j]
            result[j, :, pl.ds(h * half, half)] = piece
            squares.append(jnp.sum(piece * piece, axis=0, keepdims=True))
        return squares

    out_own = [owner_copies(h, h, to_out[h], from_out[h]) for h in range(2)]
    in_own = [owner_copies(2 + h, h, to_in[h], from_in[h]) for h in range(2)]
    for h in range(2):
        term_out_1[h].finish()
        add_terms(h, term_out[h], sum_out[h], to_out[h])
        for copy in out_own[h]:
            copy.start()
    for r in term_in_1:
        r.forward()

    def await_slots(k, _):
        slot_copy(k).wait_recv()
        return 0

    lax.fori_loop(1, GROUPS, await_slots, 0)

    def dg_copy(s):
        rows = pl.ds(pl.multiple_of(s * 2 * ROWS, 2 * ROWS), 2 * ROWS)
        return pltpu.make_async_copy(dg_v.at[rows], dg_hbm.at[rows], dg_sem.at[s])

    def apply_factor(s, _):
        tn = (((0,), (0,)), ((), ()))
        for w in range(2):
            p = pos_slot[2 * s + w]
            factor = slots[s, w]
            rows = pl.ds(pl.multiple_of((2 * s + w) * ROWS, ROWS), ROWS)
            dg_v[rows, :hd] = lax.dot_general(
                factor, tab_in[0][p >> 4, (p >> 2) & 3, p & 3], tn, preferred_element_type=F32
            ).astype(BF16)
            dg_v[rows, hd:] = lax.dot_general(
                factor, tab_in[1][(p >> 2) & 3, p >> 4, p & 3], tn, preferred_element_type=F32
            ).astype(BF16)
        dg_copy(s).start()
        return 0

    lax.fori_loop(0, GROUPS, apply_factor, 0)

    for h in range(2):
        term_in_1[h].finish()
        add_terms(h, term_in[h], sum_in[h], to_in[h])
        for copy in in_own[h]:
            copy.start()

    def find(k, found):
        at = owner_ref[k] - me * OWN
        return tuple(jnp.where(at == j, tokens_ref[k], found[j]) for j in range(OWN))

    found = lax.fori_loop(0, owner_ref.shape[0], find, (jnp.int32(1),) * OWN)
    weight = [1.0 / jnp.full((1, 128), f, jnp.int32).astype(F32) for f in found]

    def weigh(half, by):
        return [jnp.tile(by * w, (1, half // 128)) for w in weight]

    for h in range(2):
        for copy in out_own[h]:
            copy.wait_recv()
    parts = [own_sum(h, sum_out[h], from_out[h], gout_v, weigh(hf, 2.0), hf) for h in range(2)]
    save_out = pltpu.make_async_copy(gout_v, gout_hbm, loc.at[6])
    save_out.start()
    for h in range(2):
        for copy in in_own[h]:
            copy.wait_recv()
    parts += [own_sum(h, sum_in[h], from_in[h], gin_v, weigh(hd, 1.0), hd) for h in range(2)]
    save_in = pltpu.make_async_copy(gin_v, gin_hbm, loc.at[7])
    save_in.start()

    row8 = lax.broadcasted_iota(jnp.int32, (8, 128), 0)
    square = jnp.zeros((8, 128), F32)
    for j in range(OWN):
        one_sum = jnp.zeros((1, 128), F32)
        for part in parts:
            for c in range(part[j].shape[1] // 128):
                one_sum = one_sum + part[j][:, c * 128 : (c + 1) * 128]
        square = jnp.where(row8 == j, one_sum, square)
    sq_own[...] = square

    def square_copy(k):
        return remote(
            sq_own, sq_got.at[k], sq_s.at[k], sq_r.at[k], {"tensor": (t + k) % n_tensor}
        )

    over_tensor(lambda k: square_copy(k).start())
    over_tensor(lambda k: square_copy(k).wait_recv())
    total = lax.fori_loop(1, n_tensor, lambda k, acc: acc + sq_got[k], sq_own[...])
    norm_ref[...] = jnp.sqrt(jnp.broadcast_to(jnp.sum(total, axis=1, keepdims=True), (8, 128)))

    for r in in_1 + in_2 + out_1 + out_2 + term_out_1 + term_in_1:
        r.drain()
    for copies in out_own + in_own:
        for copy in copies:
            copy.wait_send()
    over_tensor(lambda k: reduce_copy(low_part, low_got, 0, k).wait_send())
    over_tensor(lambda k: spread_copy(low_all, 1, k).wait_send())
    over_tensor(lambda k: reduce_copy(fac_part, fac_got, 2, k).wait_send())
    over_tensor(lambda k: spread_copy(fac_all, 3, k).wait_send())
    over_tensor(lambda k: square_copy(k).wait_send())

    def drain_slots(k, _):
        slot_copy(k).wait_send()
        return 0

    lax.fori_loop(1, GROUPS, drain_slots, 0)

    def drain_dg(s, _):
        dg_copy(s).wait()
        return 0

    lax.fori_loop(0, GROUPS, drain_dg, 0)
    save_out.wait()
    save_in.wait()


def per_device(
    hidden_in, grad_gate, adapter_in, adapter_out, block_tenant, block_dest, tenant_tokens, tenant_owner
):
    n_tensor = lax.axis_size("tensor")
    bt = BLK // n_tensor
    cd, cf = hidden_in.shape[1], grad_gate.shape[1]
    hd, hf = cd // 2, cf // 2
    wide = SIDE * OWN * R

    def pair(shape, dtype):
        return [pltpu.VMEM(shape, dtype), pltpu.VMEM(shape, dtype)]

    dma = pltpu.SemaphoreType.DMA
    smem = pl.BlockSpec(memory_space=pltpu.SMEM)
    hbm = pl.BlockSpec(memory_space=pltpu.HBM)
    scratch = [
        pltpu.VMEM(hidden_in.shape, BF16),
        pltpu.VMEM(grad_gate.shape, BF16),
        pair((SIDE, SIDE, OWN, R, hd), BF16),
        pair((SIDE, SIDE, OWN, R, hf), BF16),
        pltpu.VMEM((BLK, R, ROWS), F32),
        pltpu.VMEM((BLK, R, ROWS), F32),
        pltpu.VMEM((n_tensor, bt, R, ROWS), F32),
        pltpu.VMEM((n_tensor, bt, R, ROWS), F32),
        pltpu.VMEM((BLK, R, ROWS), BF16),
        pltpu.VMEM((BLK, R, ROWS), BF16),
        pair((SIDE, BLK, R, hd), BF16),
        pair((SIDE, BLK, R, hf), BF16),
        pair((wide, SIDE * BLK * R), BF16),
        pair((wide, hd), F32),
        pair((wide, hf), F32),
        pair((SIDE, OWN * R, hd), BF16),
        pair((SIDE, OWN * R, hf), BF16),
        pair((SIDE - 1, OWN * R, hd), BF16),
        pair((SIDE - 1, OWN * R, hf), BF16),
        pltpu.VMEM((GROUPS, 2, R, ROWS), BF16),
        pltpu.VMEM((GROUPS, 2, R, ROWS), BF16),
        pltpu.VMEM((GROUPS * 2 * ROWS, cd), BF16),
        pltpu.VMEM((OWN, R, cd), F32),
        pltpu.VMEM((OWN, R, cf), F32),
        pltpu.VMEM((8, 128), F32),
        pltpu.VMEM((n_tensor, 8, 128), F32),
        pltpu.SMEM((BLK,), jnp.int32),
        pltpu.SMEM((2 * GROUPS,), jnp.int32),
        dma((12, 4)),
        dma((12, 4)),
        dma((4, n_tensor)),
        dma((4, n_tensor)),
        dma((GROUPS,)),
        dma((GROUPS,)),
        dma((4, SIDE - 1)),
        dma((4, SIDE - 1)),
        dma((n_tensor,)),
        dma((n_tensor,)),
        dma((8,)),
        dma((GROUPS,)),
    ]
    dgrad, grad_in, grad_out, norms = pl.pallas_call(
        functools.partial(kernel, n_tensor),
        out_shape=(
            jax.ShapeDtypeStruct((GROUPS * 2 * ROWS, cd), BF16),
            jax.ShapeDtypeStruct((OWN, R, cd), F32),
            jax.ShapeDtypeStruct((OWN, R, cf), F32),
            jax.ShapeDtypeStruct((8, 128), F32),
        ),
        in_specs=[smem] * 4 + [hbm] * 4,
        out_specs=(hbm, hbm, hbm, pl.BlockSpec(memory_space=pltpu.VMEM)),
        scratch_shapes=scratch,
        compiler_params=pltpu.CompilerParams(
            collective_id=0, has_side_effects=True, vmem_limit_bytes=60 * 1024 * 1024
        ),
    )(
        block_tenant,
        block_dest.reshape(-1),
        tenant_tokens,
        tenant_owner,
        hidden_in,
        grad_gate,
        adapter_in,
        adapter_out,
    )
    return dgrad, grad_in, grad_out, norms[:OWN, 0]


def solution(mesh):
    return jax.shard_map(
        per_device,
        mesh=mesh,
        in_specs=(
            P("dp", "tensor"),
            P("dp", "tensor"),
            P("dp", None, "tensor"),
            P("dp", None, "tensor"),
            P(),
            P(),
            P(),
            P(),
        ),
        out_specs=(P("dp", "tensor"), P("dp", None, "tensor"), P("dp", None, "tensor"), P("dp")),
        check_vma=False,
    )
```

time: 559 us -> 96.3 us (0.17)
  waiting for transfers between devices: 367 us -> 0 us
  Pallas kernels: 0 us -> 88.4 us
  blocking collectives: 83 us -> 0 us
  local copies, waits for them, and re-layouts: 47.9 us -> 7.19 us
  matrix products: 25.6 us -> 0 us
  starting transfers between devices: 14.6 us -> 0 us
  between operations: 14 us -> 0.65 us
  other arithmetic: 6.01 us -> 0 us
    all_to_all x2 -> x0, waiting for transfers between devices: 120 us -> none  [the longest x1 120 us: per_device(): lax.all_to_all(send_g, 'dp', split_axis=0, concat_axis=0, tiled=True)]
    psum x1 -> x0, waiting for transfers between devices: 114 us -> none  [rank_factors(): low_sum, backward_total = lax.psum((low_part, back_part), 'tensor')]
    reduce_scatter x2 -> x0, waiting for transfers between devices: 91.2 us -> none  [the longest x1 85 us: per_device(): lax.psum_scatter(term_out, 'dp', scatter_dimension=0, tiled=True)]
    pallas_call x0 -> x1, Pallas kernels: none -> 88.4 us  [per_device(): pl.pallas_call(functools.partial(kernel, n_tensor), out_shape=(jax.ShapeD...]
    psum x2 -> x0, blocking collectives: 83 us -> none  [the longest x1 57.3 us: rank_factors(): low_sum, backward_total = lax.psum((low_part, back_part), 'tensor')]
    all_gather x2 -> x0, waiting for transfers between devices: 40.4 us -> none  [the longest x1 40.4 us: per_device(): lax.all_gather(adapter_in, 'dp', axis=0, tiled=True)]
    dot_general x9 -> x0, matrix products: 25.6 us -> none  [the longest x1 5.67 us: rank_factors(): jnp.einsum('nbf,nrf->nbr', gradient_rows, output_matrix, preferred_elemen...]
    scatter x5 -> x0, local copies, waits for them, and re-layouts: 20.6 us -> none  [the longest x2 16.1 us: place_blocks(): return empty.at[places].set(blocks)]
  transfers between devices with their start and end apart: 7 -> 0, of which waited for: 5 -> 0; matrix products, arithmetic and copies ran while one was open for 10% -> 0% of each run, Pallas kernels for 0% -> 0%
where the time goes in v1:
time: 96.3 us; the launch traced here: 96.2 us
  Pallas kernels  88.4 us (92%)
  local copies, waits for them, and re-layouts  7.19 us (7%)
    pallas_call x1, Pallas kernels, per_device(): pl.pallas_call(functools.partial(kernel, n_tensor), out_shape=(jax.ShapeD...  88.4 us
    unnamed x7, local copies, waits for them, and re-layouts  5.89 us

profile of v1, /device:TPU:1, one launch (start us, length us, event | category | flops | bytes accessed | tf_op | source)
XLA Modules:
  0.0 96.2 jit_solution(10384293701252197973)
XLA Ops:
  0.6 88.4 %shard_map.111 = (bf16[4096,512]{1,0:T(8,128)(2,1)}, f32[4,16,512]{2,1,0:T(8,128)}, f32[4,16,1024]{2,1,0:T(8,128)}, f32[8,128]{1,0:T(8,128)}) custom-call(s32[256]{0:T(256)} %tenant_ref.1, s32[256]{0:T(256)} %bitcast.1, s32[64]{0:T(128)} %tokens_ref.1, s32[64]{0:T(128)} %owner_ref.1, bf16[2048,512]{1,0:T(8,128)(2,1)} %x_hbm.1, bf16[2048,1024]{1,0:T(8,128)(2,1)} %g_hbm.1, ...), custom_call_target="tpu_custom_call" | custom-call | tf_op jit(solution)/shard_map/pallas_call | solution.py:566
  89.0 1.3 %slice_reduce_fusion = f32[4]{0:T(128)} fusion(f32[8,128]{1,0:T(8,128)} %get-tuple-element.11), kind=kLoop, calls=%fused_computation | loop fusion | bytes 32 | tf_op jit(solution)/shard_map/slice | solution.py:590
  90.3 0.0 copy-start.1
  90.3 0.0 copy-start
  90.3 4.5 %copy.15 = bf16[4096,512]{1,0:T(8,128)(2,1)} copy(bf16[4096,512]{1,0:T(8,128)(2,1)} %get-tuple-element.16) | data formatting | bytes 8388608
  94.8 0.0 copy-done.1
  94.8 0.7 copy.16
  95.5 0.0 copy-done
  95.5 0.7 copy.17
Async XLA Ops:
  90.3 4.5 %copy-start.1 = (f32[4,16,512]{2,1,0:T(8,128)S(1)}, f32[4,16,512]{2,1,0:T(8,128)}, u32[]{:S(2)}) copy-start(f32[4,16,512]{2,1,0:T(8,128)} %get-tuple-element.17) | copy-start | bytes 393220
  90.3 5.2 %copy-start = (f32[4,16,1024]{2,1,0:T(8,128)S(1)}, f32[4,16,1024]{2,1,0:T(8,128)}, u32[]{:S(2)}) copy-start(f32[4,16,1024]{2,1,0:T(8,128)} %get-tuple-element.18) | copy-start | bytes 786436

commit v2 on v1

--- a/solution.py
+++ b/solution.py
@@ -29,40 +29,83 @@
     )
 
 
+def await_bytes(ref, sem):
+    pltpu.make_async_copy(ref, ref, sem).wait()
+
+
+class Gather:
+    def __init__(self, buf, first, second, ring, number, src):
+        a, b = first[0], second[0]
+        column = [buf.at[:, (a + k) % SIDE] for k in (0, 3, 1, 2)]
+        row = ring(number, buf.at[b], first, src, True)
+        mine = ring(number + 1, column[0], second, src, False)
+        before, after, far = [ring(number + 1 + k, column[k], second, None, False) for k in (1, 2, 3)]
+
+        def come(way, onward):
+            def step():
+                row.forward_one(way)
+                onward.start()
+
+            return step
+
+        def opposite():
+            row.finish()
+            far.start()
+
+        self.steps = [
+            [row.start, mine.start],
+            [come(0, before), come(1, after), opposite, mine.forward],
+            [before.forward, after.forward],
+            [far.forward, mine.finish],
+            [before.finish, after.finish, far.finish],
+        ]
+        self.rings = (row, mine, before, after, far)
+
+    def drain(self):
+        for r in self.rings:
+            r.drain()
+
+
 class Ring:
-    def __init__(self, buf, here, right, left, sends, recvs, src=None):
+    def __init__(self, buf, here, right, left, far, sends, recvs, src=None, direct=False):
         self.buf, self.here, self.right, self.left = buf, here, right, left
         half = buf.shape[1] // 2
         before, after = (here + 3) % SIDE, (here + 1) % SIDE
         own = buf.at[here] if src is None else src
         mine = buf.at[here]
+        self.sends, self.recvs = sends, recvs
         self.own = [
-            remote(own, mine, sends.at[0], recvs.at[0], right),
-            remote(own, mine, sends.at[1], recvs.at[1], left),
+            remote(own, mine, sends, recvs.at[0], right),
+            remote(own, mine, sends, recvs.at[1], left),
         ]
         low = buf.at[before, pl.ds(0, half)]
         high = buf.at[after, pl.ds(half, half)]
         self.pass_on = [
-            remote(low, low, sends.at[2], recvs.at[2], right),
-            remote(high, high, sends.at[3], recvs.at[3], left),
+            remote(low, low, sends, recvs.at[2], right),
+            remote(high, high, sends, recvs.at[2], left),
         ]
+        self.direct = direct
+        if direct:
+            self.own.append(remote(own, mine, sends, recvs.at[2], far))
 
     def start(self):
         for copy in self.own:
             copy.start()
 
+    def forward_one(self, way):
+        self.own[way].wait_recv()
+        if not self.direct:
+            self.pass_on[way].start()
+
     def forward(self):
-        for copy, onward in zip(self.own, self.pass_on):
-            copy.wait_recv()
-            onward.start()
+        self.forward_one(0)
+        self.forward_one(1)
 
     def finish(self):
-        for copy in self.pass_on:
-            copy.wait_recv()
+        await_bytes(self.buf.at[(self.here + 2) % SIDE], self.recvs.at[2])
 
     def drain(self):
-        for copy in self.own + self.pass_on:
-            copy.wait_send()
+        await_bytes(self.buf.at[pl.ds(0, SIDE - 1)], self.sends)
 
 
 def kernel(
@@ -75,7 +118,8 @@
     g_hbm,
     ain_hbm,
     aout_hbm,
-    dg_hbm,
+    slots_hbm,
+    sel_hbm,
     gin_hbm,
     gout_hbm,
     norm_ref,
@@ -100,7 +144,7 @@
     from_out,
     slot_send,
     slots,
-    dg_v,
+    sel_v,
     gin_v,
     gout_v,
     sq_own,
@@ -111,14 +155,11 @@
     ring_r,
     z_s,
     z_r,
-    slot_s,
-    slot_r,
+    slot_sem,
     own_s,
     own_r,
-    sq_s,
-    sq_r,
+    sq_sem,
     loc,
-    dg_sem,
 ):
     me = lax.axis_index("dp")
     t = lax.axis_index("tensor")
@@ -127,12 +168,15 @@
     cd, cf = x_v.shape[1], g_v.shape[1]
     hd, hf = cd // 2, cf // 2
 
+    ends = []
+
     def at_dp(yy, xx):
         return {"dp": yy * SIDE + xx}
 
     x_right, x_left = at_dp(y, (x + 1) % SIDE), at_dp(y, (x + 3) % SIDE)
     y_right, y_left = at_dp((y + 1) % SIDE, x), at_dp((y + 3) % SIDE, x)
-    along_x, along_y = (x, x_right, x_left), (y, y_right, y_left)
+    x_far, y_far = at_dp(y, (x + 2) % SIDE), at_dp((y + 2) % SIDE, x)
+    along_x, along_y = (x, x_right, x_left, x_far), (y, y_right, y_left, y_far)
 
     load_x = pltpu.make_async_copy(x_hbm, x_v, loc.at[0])
     load_g = pltpu.make_async_copy(g_hbm, g_v, loc.at[1])
@@ -181,24 +225,6 @@
     lax.fori_loop(0, BLK, own_places, 0)
     pl.semaphore_wait(barrier, GROUPS - 1 + n_tensor - 1)
 
-    def ring(number, buf, along, src=None):
-        return Ring(buf, along[0], along[1], along[2], ring_s.at[number], ring_r.at[number], src)
-
-    first, second = [along_x, along_y], [along_y, along_x]
-    in_1 = [ring(h, tab_in[h].at[places[h][0]], first[h], in_cols[h]) for h in range(2)]
-    in_2 = [ring(2 + h, tab_in[h], second[h]) for h in range(2)]
-    out_1 = [ring(4 + h, tab_out[h].at[places[h][0]], first[h], out_cols[h]) for h in range(2)]
-    out_2 = [ring(6 + h, tab_out[h], second[h]) for h in range(2)]
-    for r in in_1 + out_1:
-        r.start()
-    for copy in own_tables:
-        copy.wait()
-    for r in in_1 + out_1:
-        r.forward()
-    for r, after in zip(in_1 + out_1, in_2 + out_2):
-        r.finish()
-        after.start()
-
     def slot_places(s, _):
         one, two = jnp.int32(-1), jnp.int32(-1)
         for i in range(BLK):
@@ -211,7 +237,8 @@
         pos_slot[2 * s + 1] = jnp.maximum(two, 0)
         return 0
 
-    lax.fori_loop(0, GROUPS, slot_places, 0)
+    def slot_tables():
+        lax.fori_loop(0, GROUPS, slot_places, 0)
 
     def choose(q, _):
         lane = lax.broadcasted_iota(jnp.int32, (8, 128), 1)
@@ -234,8 +261,37 @@
             pick[h][:, pl.ds(pl.multiple_of(q * 128, 128), 128)] = jnp.where(hit, 1.0, 0.0).astype(BF16)
         return 0
 
-    lax.fori_loop(0, 2 * SIDE, choose, 0)
-
+    def choose_all():
+        lax.fori_loop(0, 2 * SIDE, choose, 0)
+
+    def find(k, found):
+        at = owner_ref[k] - me * OWN
+        return tuple(jnp.where(at == j, tokens_ref[k], found[j]) for j in range(OWN))
+
+    def owned_weights():
+        found = lax.fori_loop(0, owner_ref.shape[0], find, (jnp.int32(1),) * OWN)
+        return [1.0 / jnp.full((1, 128), f, jnp.int32).astype(F32) for f in found]
+
+    def ring(number, buf, along, src=None, direct=False):
+        return Ring(buf, *along, ring_s.at[number], ring_r.at[number], src, direct)
+
+    first, second = [along_x, along_y], [along_y, along_x]
+    tab_in_ag = [Gather(tab_in[h], first[h], second[h], ring, 5 * h, in_cols[h]) for h in range(2)]
+    tab_out_ag = [
+        Gather(tab_out[h], first[h], second[h], ring, 10 + 5 * h, out_cols[h]) for h in range(2)
+    ]
+
+    def deep(gathers, depth):
+        for part in range(len(gathers[0].steps[depth])):
+            for gather in gathers:
+                gather.steps[depth][part]()
+
+    for gathers in (tab_in_ag, tab_out_ag):
+        deep(gathers, 0)
+        ends.extend(g.drain for g in gathers)
+    slot_tables()
+    for copy in own_tables:
+        copy.wait()
     def partial_products(table, rows_v, half, part):
         def one(b, _):
             p = pos_own[b]
@@ -255,15 +311,15 @@
         return remote(
             part.at[pl.ds(to * bt, bt)],
             got.at[k],
-            z_s.at[number, k],
-            z_r.at[number, k],
+            z_s.at[number],
+            z_r.at[number],
             {"tensor": to},
         )
 
     def spread_copy(full, number, k):
         mine = full.at[pl.ds(t * bt, bt)]
         return remote(
-            mine, mine, z_s.at[number, k], z_r.at[number, k], {"tensor": (t + k) % n_tensor}
+            mine, mine, z_s.at[number], z_r.at[number], {"tensor": (t + k) % n_tensor}
         )
 
     def over_tensor(do):
@@ -271,60 +327,77 @@
 
     def send_parts(part, got, number):
         over_tensor(lambda k: reduce_copy(part, got, number, k).start())
+        ends.append(lambda: await_bytes(got.at[pl.ds(1, n_tensor - 1)], z_s.at[number]))
 
     def add_parts(part, got, full, number, scale):
-        over_tensor(lambda k: reduce_copy(part, got, number, k).wait_recv())
+        await_bytes(got.at[pl.ds(1, n_tensor - 1)], z_r.at[number])
         total = lax.fori_loop(1, n_tensor, lambda k, acc: acc + got[k], part[pl.ds(t * bt, bt)])
         full[pl.ds(t * bt, bt)] = (scale * total).astype(BF16)
         over_tensor(lambda k: spread_copy(full, number + 1, k).start())
+        ends.append(lambda: await_bytes(full.at[pl.ds(0, BLK - bt)], z_s.at[number + 1]))
 
     def take_spread(full, number):
-        over_tensor(lambda k: spread_copy(full, number, k).wait_recv())
-
-    def terms(factor, rows_v, half, out):
-        for h in range(2):
-
-            def one(b, _):
-                rows = rows_v[pl.ds(pl.multiple_of(b * ROWS, ROWS), ROWS), pl.ds(h * half, half)]
-                out[h][first[h][0], b] = jnp.dot(
-                    factor[b], rows, preferred_element_type=F32
-                ).astype(BF16)
-                return 0
-
-            lax.fori_loop(0, BLK, one, 0, unroll=2)
-
-    for r in in_2:
-        r.forward()
-    for r in in_2:
-        r.finish()
+        await_bytes(full.at[pl.ds(0, BLK - bt)], z_r.at[number])
+
+    def terms(h, factor, rows_v, half, out):
+        def one(b, _):
+            rows = rows_v[pl.ds(pl.multiple_of(b * ROWS, ROWS), ROWS), pl.ds(h * half, half)]
+            out[h][first[h][0], b] = jnp.dot(
+                factor[b], rows, preferred_element_type=F32
+            ).astype(BF16)
+            return 0
+
+        lax.fori_loop(0, BLK, one, 0, unroll=2)
+
+    def select(i, _):
+        p = pos_slot[i]
+        sel_v[i, :, :hd] = tab_in[0][p >> 4, (p >> 2) & 3, p & 3]
+        sel_v[i, :, hd:] = tab_in[1][(p >> 2) & 3, p >> 4, p & 3]
+        return 0
+
+    def select_all():
+        lax.fori_loop(0, 2 * GROUPS, select, 0, unroll=4)
+        save_sel = pltpu.make_async_copy(sel_v, sel_hbm, loc.at[0])
+        save_sel.start()
+        ends.append(save_sel.wait)
+
+    deep(tab_in_ag, 1)
+    deep(tab_out_ag, 1)
+    deep(tab_in_ag, 2)
+    deep(tab_in_ag, 3)
+    deep(tab_out_ag, 2)
+    deep(tab_in_ag, 4)
     load_x.wait()
     partial_products(tab_in, x_v, hd, low_part)
     send_parts(low_part, low_got, 0)
-    for r in out_2:
-        r.forward()
+    select_all()
+    deep(tab_out_ag, 3)
+    choose_all()
     add_parts(low_part, low_got, low_all, 0, 1.0)
     load_g.wait()
-    take_spread(low_all, 1)
-    term_out_1 = [ring(8 + h, term_out[h], first[h]) for h in range(2)]
-    terms(low_all, g_v, hf, term_out)
-    for r in term_out_1:
-        r.start()
-    for r in out_2:
-        r.finish()
+    deep(tab_out_ag, 4)
     partial_products(tab_out, g_v, hf, fac_part)
     send_parts(fac_part, fac_got, 2)
+    take_spread(low_all, 1)
+    term_out_1 = [ring(20 + h, term_out[h], first[h], None, False) for h in range(2)]
+    for h in range(2):
+        terms(h, low_all, g_v, hf, term_out)
+        term_out_1[h].start()
+        ends.append(term_out_1[h].drain)
+    add_parts(fac_part, fac_got, fac_all, 2, 2.0)
     for r in term_out_1:
         r.forward()
-    add_parts(fac_part, fac_got, fac_all, 2, 2.0)
+    weight = owned_weights()
     take_spread(fac_all, 3)
-    term_in_1 = [ring(10 + h, term_in[h], first[h]) for h in range(2)]
-    terms(fac_all, x_v, hd, term_in)
-    for r in term_in_1:
-        r.start()
+    term_in_1 = [ring(22 + h, term_in[h], first[h], None, False) for h in range(2)]
+    for h in range(2):
+        terms(h, fac_all, x_v, hd, term_in)
+        term_in_1[h].start()
+        ends.append(term_in_1[h].drain)
 
     def slot_copy(k):
         to = (me + k) % GROUPS
-        return remote(slot_send.at[k], slots.at[me], slot_s.at[k], slot_r.at[k], {"dp": to})
+        return remote(slot_send.at[k], slots.at[me], slot_sem.at[0], slot_sem.at[1], {"dp": to})
 
     def blocks_for(group):
         one, two = jnp.int32(-1), jnp.int32(-1)
@@ -346,6 +419,8 @@
         return 0
 
     lax.fori_loop(1, GROUPS, pack, 0)
+
+    ends.append(lambda: await_bytes(slots.at[pl.ds(0, GROUPS - 1)], slot_sem.at[0]))
     one, two = blocks_for(me)
     slots[me, 0] = masked(one)
     slots[me, 1] = masked(two)
@@ -360,8 +435,8 @@
                 remote(
                     sends.at[to],
                     lands.at[k - 1],
-                    own_s.at[number, k - 1],
-                    own_r.at[number, k - 1],
+                    own_s.at[number],
+                    own_r.at[number],
                     device,
                 )
             )
@@ -404,32 +479,10 @@
     for r in term_in_1:
         r.forward()
 
-    def await_slots(k, _):
-        slot_copy(k).wait_recv()
-        return 0
-
-    lax.fori_loop(1, GROUPS, await_slots, 0)
-
-    def dg_copy(s):
-        rows = pl.ds(pl.multiple_of(s * 2 * ROWS, 2 * ROWS), 2 * ROWS)
-        return pltpu.make_async_copy(dg_v.at[rows], dg_hbm.at[rows], dg_sem.at[s])
-
-    def apply_factor(s, _):
-        tn = (((0,), (0,)), ((), ()))
-        for w in range(2):
-            p = pos_slot[2 * s + w]
-            factor = slots[s, w]
-            rows = pl.ds(pl.multiple_of((2 * s + w) * ROWS, ROWS), ROWS)
-            dg_v[rows, :hd] = lax.dot_general(
-                factor, tab_in[0][p >> 4, (p >> 2) & 3, p & 3], tn, preferred_element_type=F32
-            ).astype(BF16)
-            dg_v[rows, hd:] = lax.dot_general(
-                factor, tab_in[1][(p >> 2) & 3, p >> 4, p & 3], tn, preferred_element_type=F32
-            ).astype(BF16)
-        dg_copy(s).start()
-        return 0
-
-    lax.fori_loop(0, GROUPS, apply_factor, 0)
+    await_bytes(slots.at[pl.ds(0, GROUPS - 1)], slot_sem.at[1])
+    save_slots = pltpu.make_async_copy(slots, slots_hbm, loc.at[1])
+    save_slots.start()
+    ends.append(save_slots.wait)
 
     for h in range(2):
         term_in_1[h].finish()
@@ -437,28 +490,25 @@
         for copy in in_own[h]:
             copy.start()
 
-    def find(k, found):
-        at = owner_ref[k] - me * OWN
-        return tuple(jnp.where(at == j, tokens_ref[k], found[j]) for j in range(OWN))
-
-    found = lax.fori_loop(0, owner_ref.shape[0], find, (jnp.int32(1),) * OWN)
-    weight = [1.0 / jnp.full((1, 128), f, jnp.int32).astype(F32) for f in found]
-
     def weigh(half, by):
         return [jnp.tile(by * w, (1, half // 128)) for w in weight]
 
     for h in range(2):
-        for copy in out_own[h]:
-            copy.wait_recv()
+        await_bytes(from_out[h], own_r.at[h])
     parts = [own_sum(h, sum_out[h], from_out[h], gout_v, weigh(hf, 2.0), hf) for h in range(2)]
     save_out = pltpu.make_async_copy(gout_v, gout_hbm, loc.at[6])
     save_out.start()
-    for h in range(2):
-        for copy in in_own[h]:
-            copy.wait_recv()
+    ends.append(save_out.wait)
+    for h in range(2):
+        await_bytes(from_in[h], own_r.at[2 + h])
     parts += [own_sum(h, sum_in[h], from_in[h], gin_v, weigh(hd, 1.0), hd) for h in range(2)]
     save_in = pltpu.make_async_copy(gin_v, gin_hbm, loc.at[7])
     save_in.start()
+    ends.append(save_in.wait)
+
+    for h in range(2):
+        ends.append(functools.partial(await_bytes, from_out[h], own_s.at[h]))
+        ends.append(functools.partial(await_bytes, from_in[h], own_s.at[2 + h]))
 
     row8 = lax.broadcasted_iota(jnp.int32, (8, 128), 0)
     square = jnp.zeros((8, 128), F32)
@@ -472,38 +522,59 @@
 
     def square_copy(k):
         return remote(
-            sq_own, sq_got.at[k], sq_s.at[k], sq_r.at[k], {"tensor": (t + k) % n_tensor}
+            sq_own, sq_got.at[k], sq_sem.at[0], sq_sem.at[1], {"tensor": (t + k) % n_tensor}
         )
 
     over_tensor(lambda k: square_copy(k).start())
-    over_tensor(lambda k: square_copy(k).wait_recv())
+    ends.append(lambda: await_bytes(sq_got.at[pl.ds(1, n_tensor - 1)], sq_sem.at[0]))
+    await_bytes(sq_got.at[pl.ds(1, n_tensor - 1)], sq_sem.at[1])
     total = lax.fori_loop(1, n_tensor, lambda k, acc: acc + sq_got[k], sq_own[...])
     norm_ref[...] = jnp.sqrt(jnp.broadcast_to(jnp.sum(total, axis=1, keepdims=True), (8, 128)))
 
-    for r in in_1 + in_2 + out_1 + out_2 + term_out_1 + term_in_1:
-        r.drain()
-    for copies in out_own + in_own:
-        for copy in copies:
-            copy.wait_send()
-    over_tensor(lambda k: reduce_copy(low_part, low_got, 0, k).wait_send())
-    over_tensor(lambda k: spread_copy(low_all, 1, k).wait_send())
-    over_tensor(lambda k: reduce_copy(fac_part, fac_got, 2, k).wait_send())
-    over_tensor(lambda k: spread_copy(fac_all, 3, k).wait_send())
-    over_tensor(lambda k: square_copy(k).wait_send())
-
-    def drain_slots(k, _):
-        slot_copy(k).wait_send()
-        return 0
-
-    lax.fori_loop(1, GROUPS, drain_slots, 0)
-
-    def drain_dg(s, _):
-        dg_copy(s).wait()
-        return 0
-
-    lax.fori_loop(0, GROUPS, drain_dg, 0)
-    save_out.wait()
-    save_in.wait()
+    for end in ends:
+        end()
+
+
+def place(
+    slots, sel, gin, gout, norms, dg_to, gin_to, gout_to, norms_to, slots_v, sel_v, dg_v, gin_v, gout_v, sems
+):
+    cd = dg_v.shape[1]
+    quarter = 2 * GROUPS // 4
+    load_slots = pltpu.make_async_copy(slots, slots_v, sems.at[0])
+    load_slots.start()
+    load_sel = []
+    for i in range(4):
+        some = pl.ds(i * quarter, quarter)
+        load_sel.append(pltpu.make_async_copy(sel.at[some], sel_v.at[some], sems.at[1 + i]))
+        load_sel[i].start()
+    moves = [(gin, gin_v, gin_to), (gout, gout_v, gout_to)]
+    loads = [pltpu.make_async_copy(m[0], m[1], sems.at[5 + i]) for i, m in enumerate(moves)]
+    saves = [pltpu.make_async_copy(m[1], m[2], sems.at[7 + i]) for i, m in enumerate(moves)]
+    for copy in loads:
+        copy.start()
+    for j in range(OWN):
+        norms_to[j] = norms[j, 0]
+    load_slots.wait()
+    for i in range(4):
+        load_sel[i].wait()
+
+        def one(k, _):
+            slot = i * quarter + k
+            rows = pl.ds(pl.multiple_of(slot * ROWS, ROWS), ROWS)
+            dg_v[rows, :] = lax.dot_general(
+                slots_v[slot], sel_v[slot], (((0,), (0,)), ((), ())), preferred_element_type=F32
+            ).astype(BF16)
+            return 0
+
+        lax.fori_loop(0, quarter, one, 0, unroll=4)
+        rows = pl.ds(i * quarter * ROWS, quarter * ROWS)
+        saves.append(pltpu.make_async_copy(dg_v.at[rows], dg_to.at[rows], sems.at[9 + i]))
+        saves[-1].start()
+    for load, save in zip(loads, saves):
+        load.wait()
+        save.start()
+    for copy in saves:
+        copy.wait()
 
 
 def per_device(
@@ -543,36 +614,34 @@
         pair((SIDE - 1, OWN * R, hf), BF16),
         pltpu.VMEM((GROUPS, 2, R, ROWS), BF16),
         pltpu.VMEM((GROUPS, 2, R, ROWS), BF16),
-        pltpu.VMEM((GROUPS * 2 * ROWS, cd), BF16),
+        pltpu.VMEM((2 * GROUPS, R, cd), BF16),
         pltpu.VMEM((OWN, R, cd), F32),
         pltpu.VMEM((OWN, R, cf), F32),
         pltpu.VMEM((8, 128), F32),
         pltpu.VMEM((n_tensor, 8, 128), F32),
         pltpu.SMEM((BLK,), jnp.int32),
         pltpu.SMEM((2 * GROUPS,), jnp.int32),
-        dma((12, 4)),
-        dma((12, 4)),
-        dma((4, n_tensor)),
-        dma((4, n_tensor)),
-        dma((GROUPS,)),
-        dma((GROUPS,)),
-        dma((4, SIDE - 1)),
-        dma((4, SIDE - 1)),
-        dma((n_tensor,)),
-        dma((n_tensor,)),
+        dma((24,)),
+        dma((24, 3)),
+        dma((4,)),
+        dma((4,)),
+        dma((2,)),
+        dma((4,)),
+        dma((4,)),
+        dma((2,)),
         dma((8,)),
-        dma((GROUPS,)),
     ]
-    dgrad, grad_in, grad_out, norms = pl.pallas_call(
+    results = pl.pallas_call(
         functools.partial(kernel, n_tensor),
         out_shape=(
-            jax.ShapeDtypeStruct((GROUPS * 2 * ROWS, cd), BF16),
+            jax.ShapeDtypeStruct((GROUPS, 2, R, ROWS), BF16),
+            jax.ShapeDtypeStruct((2 * GROUPS, R, cd), BF16),
             jax.ShapeDtypeStruct((OWN, R, cd), F32),
             jax.ShapeDtypeStruct((OWN, R, cf), F32),
             jax.ShapeDtypeStruct((8, 128), F32),
         ),
         in_specs=[smem] * 4 + [hbm] * 4,
-        out_specs=(hbm, hbm, hbm, pl.BlockSpec(memory_space=pltpu.VMEM)),
+        out_specs=(hbm, hbm, hbm, hbm, pl.BlockSpec(memory_space=pltpu.VMEM)),
         scratch_shapes=scratch,
         compiler_params=pltpu.CompilerParams(
             collective_id=0, has_side_effects=True, vmem_limit_bytes=60 * 1024 * 1024
@@ -587,7 +656,27 @@
         adapter_in,
         adapter_out,
     )
-    return dgrad, grad_in, grad_out, norms[:OWN, 0]
+    slots, sel, grad_in, grad_out, norms = results
+    return pl.pallas_call(
+        place,
+        out_shape=(
+            jax.ShapeDtypeStruct((GROUPS * 2 * ROWS, cd), BF16),
+            jax.ShapeDtypeStruct((OWN, R, cd), F32),
+            jax.ShapeDtypeStruct((OWN, R, cf), F32),
+            jax.ShapeDtypeStruct((OWN,), F32),
+        ),
+        in_specs=[hbm] * 4 + [smem],
+        out_specs=(hbm, hbm, hbm, smem),
+        scratch_shapes=[
+            pltpu.VMEM((2 * GROUPS, R, ROWS), BF16),
+            pltpu.VMEM((2 * GROUPS, R, cd), BF16),
+            pltpu.VMEM((GROUPS * 2 * ROWS, cd), BF16),
+            pltpu.VMEM((OWN, R, cd), F32),
+            pltpu.VMEM((OWN, R, cf), F32),
+            dma((13,)),
+        ],
+        compiler_params=pltpu.CompilerParams(vmem_limit_bytes=60 * 1024 * 1024),
+    )(slots.reshape(2 * GROUPS, R, ROWS), sel, grad_in, grad_out, norms)
 
 
 def solution(mesh):

time: 96.3 us -> 83.2 us (0.86)
  local copies, waits for them, and re-layouts: 7.19 us -> 0 us
  Pallas kernels: 88.4 us -> 82.4 us
    pallas_call x1, Pallas kernels: 88.4 us -> 76.4 us  [per_device(): pl.pallas_call(functools.partial(kernel, n_tensor), out_shape=(jax.ShapeD...]
    pallas_call x0 -> x1, Pallas kernels: none -> 5.97 us  [per_device(): pl.pallas_call(place, out_shape=(jax.ShapeDtypeStruct((GROUPS * 2 * ROWS,...]
    unnamed x7 -> x0, local copies, waits for them, and re-layouts: 5.89 us -> none
    slice x1 -> x0, local copies, waits for them, and re-layouts: 1.3 us -> none  [per_device(): return (dgrad, grad_in, grad_out, norms[:OWN, 0])]
where the time goes in v2:
time: 83.2 us; the launch traced here: 83.1 us
  Pallas kernels  82.4 us (99%)
    pallas_call x1, Pallas kernels, per_device(): pl.pallas_call(functools.partial(kernel, n_tensor), out_shape=(jax.ShapeD...  76.4 us
    pallas_call x1, Pallas kernels, per_device(): pl.pallas_call(place, out_shape=(jax.ShapeDtypeStruct((GROUPS * 2 * ROWS,...  5.97 us

profile of v2, /device:TPU:1, one launch (start us, length us, event | category | flops | bytes accessed | tf_op | source)
XLA Modules:
  0.0 83.1 jit_solution(11996405054194939445)
XLA Ops:
  0.6 76.4 %shard_map.111 = (bf16[16,2,16,128]{3,2,1,0:T(8,128)(2,1)}, bf16[32,16,512]{2,1,0:T(8,128)(2,1)}, f32[4,16,512]{2,1,0:T(8,128)}, f32[4,16,1024]{2,1,0:T(8,128)}, f32[8,128]{1,0:T(8,128)}) custom-call(s32[256]{0:T(256)} %tenant_ref.1, s32[256]{0:T(256)} %bitcast.3, s32[64]{0:T(128)} %tokens_ref.1, s32[64]{0:T(128)} %owner_ref.1, bf16[2048,512]{1,0:T(8,128)(2,1)} %x_hbm.1, ...), custom_call_target="tpu_custom_call" | custom-call | tf_op jit(solution)/shard_map/pallas_call | solution.py:634
  77.1 6.0 %shard_map.112 = (bf16[4096,512]{1,0:T(8,128)(2,1)}, f32[4,16,512]{2,1,0:T(8,128)}, f32[4,16,1024]{2,1,0:T(8,128)}, f32[4]{0:T(128)}) custom-call(bf16[32,16,128]{2,1,0:T(8,128)(2,1)} %bitcast.2, bf16[32,16,512]{2,1,0:T(8,128)(2,1)} %get-tuple-element.10.sel, f32[4,16,512]{2,1,0:T(8,128)} %get-tuple-element.11.gin, f32[4,16,1024]{2,1,0:T(8,128)} %get-tuple-element.12.gout, ...), custom_call_target="tpu_custom_call" | custom-call | tf_op jit(solution)/shard_map/pallas_call | solution.py:660

commit v3 on v2

--- a/solution.py
+++ b/solution.py
@@ -110,19 +110,22 @@
 
 def kernel(
     n_tensor,
+    tenant_hbm,
+    dest_hbm,
+    tokens_hbm,
+    owner_hbm,
+    x_hbm,
+    g_hbm,
+    ain_hbm,
+    aout_hbm,
+    dg_v,
+    gin_v,
+    gout_v,
+    norm_ref,
     tenant_ref,
     dest_ref,
     tokens_ref,
     owner_ref,
-    x_hbm,
-    g_hbm,
-    ain_hbm,
-    aout_hbm,
-    slots_hbm,
-    sel_hbm,
-    gin_hbm,
-    gout_hbm,
-    norm_ref,
     x_v,
     g_v,
     tab_in,
@@ -144,9 +147,6 @@
     from_out,
     slot_send,
     slots,
-    sel_v,
-    gin_v,
-    gout_v,
     sq_own,
     sq_got,
     pos_own,
@@ -178,8 +178,8 @@
     x_far, y_far = at_dp(y, (x + 2) % SIDE), at_dp((y + 2) % SIDE, x)
     along_x, along_y = (x, x_right, x_left, x_far), (y, y_right, y_left, y_far)
 
-    load_x = pltpu.make_async_copy(x_hbm, x_v, loc.at[0])
-    load_g = pltpu.make_async_copy(g_hbm, g_v, loc.at[1])
+    load_x = pltpu.make_async_copy(x_hbm, x_v, loc.at[8])
+    load_g = pltpu.make_async_copy(g_hbm, g_v, loc.at[9])
     in_cols = [ain_hbm.at[:, :, pl.ds(h * hd, hd)] for h in range(2)]
     out_cols = [aout_hbm.at[:, :, pl.ds(h * hf, hf)] for h in range(2)]
     places = [(y, x), (x, y)]
@@ -193,7 +193,13 @@
                 out_cols[h], tab_out[h].at[places[h][0], places[h][1]], loc.at[4 + h]
             )
         )
-    for copy in own_tables:
+    plan = [
+        pltpu.make_async_copy(tenant_hbm, tenant_ref, loc.at[0]),
+        pltpu.make_async_copy(owner_hbm, owner_ref, loc.at[1]),
+        pltpu.make_async_copy(dest_hbm, dest_ref, loc.at[6]),
+        pltpu.make_async_copy(tokens_hbm, tokens_ref, loc.at[7]),
+    ]
+    for copy in plan + own_tables:
         copy.start()
     load_x.start()
     load_g.start()
@@ -222,6 +228,8 @@
         pos_own[b] = place_of(me * BLK + b)
         return 0
 
+    for copy in plan:
+        copy.wait()
     lax.fori_loop(0, BLK, own_places, 0)
     pl.semaphore_wait(barrier, GROUPS - 1 + n_tensor - 1)
 
@@ -286,12 +294,6 @@
             for gather in gathers:
                 gather.steps[depth][part]()
 
-    for gathers in (tab_in_ag, tab_out_ag):
-        deep(gathers, 0)
-        ends.extend(g.drain for g in gathers)
-    slot_tables()
-    for copy in own_tables:
-        copy.wait()
     def partial_products(table, rows_v, half, part):
         def one(b, _):
             p = pos_own[b]
@@ -349,33 +351,27 @@
 
         lax.fori_loop(0, BLK, one, 0, unroll=2)
 
-    def select(i, _):
-        p = pos_slot[i]
-        sel_v[i, :, :hd] = tab_in[0][p >> 4, (p >> 2) & 3, p & 3]
-        sel_v[i, :, hd:] = tab_in[1][(p >> 2) & 3, p >> 4, p & 3]
-        return 0
-
-    def select_all():
-        lax.fori_loop(0, 2 * GROUPS, select, 0, unroll=4)
-        save_sel = pltpu.make_async_copy(sel_v, sel_hbm, loc.at[0])
-        save_sel.start()
-        ends.append(save_sel.wait)
-
+    for gathers in (tab_in_ag, tab_out_ag):
+        ends.extend(g.drain for g in gathers)
+    deep(tab_in_ag, 0)
+    deep(tab_out_ag, 0)
+    slot_tables()
     deep(tab_in_ag, 1)
-    deep(tab_out_ag, 1)
     deep(tab_in_ag, 2)
     deep(tab_in_ag, 3)
-    deep(tab_out_ag, 2)
     deep(tab_in_ag, 4)
+    for copy in own_tables:
+        copy.wait()
     load_x.wait()
     partial_products(tab_in, x_v, hd, low_part)
     send_parts(low_part, low_got, 0)
-    select_all()
-    deep(tab_out_ag, 3)
+    deep(tab_out_ag, 1)
+    deep(tab_out_ag, 2)
     choose_all()
     add_parts(low_part, low_got, low_all, 0, 1.0)
+    deep(tab_out_ag, 3)
+    deep(tab_out_ag, 4)
     load_g.wait()
-    deep(tab_out_ag, 4)
     partial_products(tab_out, g_v, hf, fac_part)
     send_parts(fac_part, fac_got, 2)
     take_spread(low_all, 1)
@@ -480,9 +476,21 @@
         r.forward()
 
     await_bytes(slots.at[pl.ds(0, GROUPS - 1)], slot_sem.at[1])
-    save_slots = pltpu.make_async_copy(slots, slots_hbm, loc.at[1])
-    save_slots.start()
-    ends.append(save_slots.wait)
+
+    def apply_factor(i, _):
+        p = pos_slot[i]
+        factor = slots[i // 2, i % 2]
+        rows = pl.ds(pl.multiple_of(i * ROWS, ROWS), ROWS)
+        tn = (((0,), (0,)), ((), ()))
+        dg_v[rows, :hd] = lax.dot_general(
+            factor, tab_in[0][p >> 4, (p >> 2) & 3, p & 3], tn, preferred_element_type=F32
+        ).astype(BF16)
+        dg_v[rows, hd:] = lax.dot_general(
+            factor, tab_in[1][(p >> 2) & 3, p >> 4, p & 3], tn, preferred_element_type=F32
+        ).astype(BF16)
+        return 0
+
+    lax.fori_loop(0, 2 * GROUPS, apply_factor, 0, unroll=4)
 
     for h in range(2):
         term_in_1[h].finish()
@@ -496,15 +504,9 @@
     for h in range(2):
         await_bytes(from_out[h], own_r.at[h])
     parts = [own_sum(h, sum_out[h], from_out[h], gout_v, weigh(hf, 2.0), hf) for h in range(2)]
-    save_out = pltpu.make_async_copy(gout_v, gout_hbm, loc.at[6])
-    save_out.start()
-    ends.append(save_out.wait)
     for h in range(2):
         await_bytes(from_in[h], own_r.at[2 + h])
     parts += [own_sum(h, sum_in[h], from_in[h], gin_v, weigh(hd, 1.0), hd) for h in range(2)]
-    save_in = pltpu.make_async_copy(gin_v, gin_hbm, loc.at[7])
-    save_in.start()
-    ends.append(save_in.wait)
 
     for h in range(2):
         ends.append(functools.partial(await_bytes, from_out[h], own_s.at[h]))
@@ -535,45 +537,18 @@
         end()
 
 
-def place(
-    slots, sel, gin, gout, norms, dg_to, gin_to, gout_to, norms_to, slots_v, sel_v, dg_v, gin_v, gout_v, sems
-):
-    cd = dg_v.shape[1]
-    quarter = 2 * GROUPS // 4
-    load_slots = pltpu.make_async_copy(slots, slots_v, sems.at[0])
-    load_slots.start()
-    load_sel = []
+def place(dg, gin, gout, norms, dg_to, gin_to, gout_to, norms_to, sems):
+    quarter = dg.shape[0] // 4
+    moves = [(gin, gin_to), (gout, gout_to)]
     for i in range(4):
-        some = pl.ds(i * quarter, quarter)
-        load_sel.append(pltpu.make_async_copy(sel.at[some], sel_v.at[some], sems.at[1 + i]))
-        load_sel[i].start()
-    moves = [(gin, gin_v, gin_to), (gout, gout_v, gout_to)]
-    loads = [pltpu.make_async_copy(m[0], m[1], sems.at[5 + i]) for i, m in enumerate(moves)]
-    saves = [pltpu.make_async_copy(m[1], m[2], sems.at[7 + i]) for i, m in enumerate(moves)]
-    for copy in loads:
+        rows = pl.ds(i * quarter, quarter)
+        moves.append((dg.at[rows], dg_to.at[rows]))
+    copies = [pltpu.make_async_copy(a, b, sems.at[i]) for i, (a, b) in enumerate(moves)]
+    for copy in copies:
         copy.start()
     for j in range(OWN):
         norms_to[j] = norms[j, 0]
-    load_slots.wait()
-    for i in range(4):
-        load_sel[i].wait()
-
-        def one(k, _):
-            slot = i * quarter + k
-            rows = pl.ds(pl.multiple_of(slot * ROWS, ROWS), ROWS)
-            dg_v[rows, :] = lax.dot_general(
-                slots_v[slot], sel_v[slot], (((0,), (0,)), ((), ())), preferred_element_type=F32
-            ).astype(BF16)
-            return 0
-
-        lax.fori_loop(0, quarter, one, 0, unroll=4)
-        rows = pl.ds(i * quarter * ROWS, quarter * ROWS)
-        saves.append(pltpu.make_async_copy(dg_v.at[rows], dg_to.at[rows], sems.at[9 + i]))
-        saves[-1].start()
-    for load, save in zip(loads, saves):
-        load.wait()
-        save.start()
-    for copy in saves:
+    for copy in copies:
         copy.wait()
 
 
@@ -592,7 +567,12 @@
     dma = pltpu.SemaphoreType.DMA
     smem = pl.BlockSpec(memory_space=pltpu.SMEM)
     hbm = pl.BlockSpec(memory_space=pltpu.HBM)
+    vmem = pl.BlockSpec(memory_space=pltpu.VMEM)
     scratch = [
+        pltpu.SMEM(block_tenant.shape, jnp.int32),
+        pltpu.SMEM(block_tenant.shape, jnp.int32),
+        pltpu.SMEM(tenant_tokens.shape, jnp.int32),
+        pltpu.SMEM(tenant_owner.shape, jnp.int32),
         pltpu.VMEM(hidden_in.shape, BF16),
         pltpu.VMEM(grad_gate.shape, BF16),
         pair((SIDE, SIDE, OWN, R, hd), BF16),
@@ -614,9 +594,6 @@
         pair((SIDE - 1, OWN * R, hf), BF16),
         pltpu.VMEM((GROUPS, 2, R, ROWS), BF16),
         pltpu.VMEM((GROUPS, 2, R, ROWS), BF16),
-        pltpu.VMEM((2 * GROUPS, R, cd), BF16),
-        pltpu.VMEM((OWN, R, cd), F32),
-        pltpu.VMEM((OWN, R, cf), F32),
         pltpu.VMEM((8, 128), F32),
         pltpu.VMEM((n_tensor, 8, 128), F32),
         pltpu.SMEM((BLK,), jnp.int32),
@@ -629,34 +606,37 @@
         dma((4,)),
         dma((4,)),
         dma((2,)),
-        dma((8,)),
+        dma((10,)),
     ]
     results = pl.pallas_call(
         functools.partial(kernel, n_tensor),
         out_shape=(
-            jax.ShapeDtypeStruct((GROUPS, 2, R, ROWS), BF16),
-            jax.ShapeDtypeStruct((2 * GROUPS, R, cd), BF16),
+            jax.ShapeDtypeStruct((GROUPS * 2 * ROWS, cd), BF16),
             jax.ShapeDtypeStruct((OWN, R, cd), F32),
             jax.ShapeDtypeStruct((OWN, R, cf), F32),
             jax.ShapeDtypeStruct((8, 128), F32),
         ),
-        in_specs=[smem] * 4 + [hbm] * 4,
-        out_specs=(hbm, hbm, hbm, hbm, pl.BlockSpec(memory_space=pltpu.VMEM)),
+        in_specs=[hbm] * 8,
+        out_specs=(vmem,) * 4,
         scratch_shapes=scratch,
         compiler_params=pltpu.CompilerParams(
-            collective_id=0, has_side_effects=True, vmem_limit_bytes=60 * 1024 * 1024
+            collective_id=0, has_side_effects=True, vmem_limit_bytes=40 * 1024 * 1024
         ),
     )(
-        block_tenant,
-        block_dest.reshape(-1),
-        tenant_tokens,
-        tenant_owner,
-        hidden_in,
-        grad_gate,
-        adapter_in,
-        adapter_out,
+        *(
+            pltpu.with_memory_space_constraint(a, pltpu.HBM)
+            for a in (
+                block_tenant,
+                block_dest.reshape(-1),
+                tenant_tokens,
+                tenant_owner,
+                hidden_in,
+                grad_gate,
+                adapter_in,
+                adapter_out,
+            )
+        )
     )
-    slots, sel, grad_in, grad_out, norms = results
     return pl.pallas_call(
         place,
         out_shape=(
@@ -665,18 +645,11 @@
             jax.ShapeDtypeStruct((OWN, R, cf), F32),
             jax.ShapeDtypeStruct((OWN,), F32),
         ),
-        in_specs=[hbm] * 4 + [smem],
+        in_specs=[vmem, vmem, vmem, smem],
         out_specs=(hbm, hbm, hbm, smem),
-        scratch_shapes=[
-            pltpu.VMEM((2 * GROUPS, R, ROWS), BF16),
-            pltpu.VMEM((2 * GROUPS, R, cd), BF16),
-            pltpu.VMEM((GROUPS * 2 * ROWS, cd), BF16),
-            pltpu.VMEM((OWN, R, cd), F32),
-            pltpu.VMEM((OWN, R, cf), F32),
-            dma((13,)),
-        ],
-        compiler_params=pltpu.CompilerParams(vmem_limit_bytes=60 * 1024 * 1024),
-    )(slots.reshape(2 * GROUPS, R, ROWS), sel, grad_in, grad_out, norms)
+        scratch_shapes=[dma((6,))],
+        compiler_params=pltpu.CompilerParams(vmem_limit_bytes=16 * 1024 * 1024),
+    )(*results)
 
 
 def solution(mesh):

time: 83.2 us -> 78.2 us (0.940)
  Pallas kernels: 82.4 us -> 77.5 us
    pallas_call x1, Pallas kernels: 5.97 us -> 3.3 us  [per_device(): pl.pallas_call(place, out_shape=(jax.ShapeDtypeStruct((GROUPS * 2 * ROWS,...]
    pallas_call x1, Pallas kernels: 76.4 us -> 74.2 us  [per_device(): pl.pallas_call(functools.partial(kernel, n_tensor), out_shape=(jax.ShapeD...]
where the time goes in v3:
time: 78.2 us
  Pallas kernels  77.5 us (99%)
    pallas_call x1, Pallas kernels, per_device(): pl.pallas_call(functools.partial(kernel, n_tensor), out_shape=(jax.ShapeD...  74.2 us
    pallas_call x1, Pallas kernels, per_device(): pl.pallas_call(place, out_shape=(jax.ShapeDtypeStruct((GROUPS * 2 * ROWS,...  3.3 us

profile of v3, /device:TPU:1, one launch (start us, length us, event | category | flops | bytes accessed | tf_op | source)
XLA Modules:
  0.0 78.2 jit_solution(4021387653164968477)
XLA Ops:
  0.6 74.2 %shard_map.111 = (bf16[4096,512]{1,0:T(8,128)(2,1)S(1)}, f32[4,16,512]{2,1,0:T(8,128)S(1)}, f32[4,16,1024]{2,1,0:T(8,128)S(1)}, f32[8,128]{1,0:T(8,128)S(1)}) custom-call(s32[256]{0:T(256)} %tenant_hbm.1, s32[256]{0:T(256)} %bitcast.1, s32[64]{0:T(128)} %tokens_hbm.1, s32[64]{0:T(128)} %owner_hbm.1, bf16[2048,512]{1,0:T(8,128)(2,1)} %x_hbm.1, ...), custom_call_target="tpu_custom_call" | custom-call | tf_op jit(solution)/shard_map/pallas_call | solution.py:611
  74.8 3.3 %shard_map.112 = (bf16[4096,512]{1,0:T(8,128)(2,1)}, f32[4,16,512]{2,1,0:T(8,128)}, f32[4,16,1024]{2,1,0:T(8,128)}, f32[4]{0:T(128)}) custom-call(bf16[4096,512]{1,0:T(8,128)(2,1)S(1)} %get-tuple-element.8.dg, f32[4,16,512]{2,1,0:T(8,128)S(1)} %get-tuple-element.9.gin, f32[4,16,1024]{2,1,0:T(8,128)S(1)} %get-tuple-element.10.gout, ...), custom_call_target="tpu_custom_call" | custom-call | tf_op jit(solution)/shard_map/pallas_call | solution.py:640

commit v4 on v3

--- a/solution.py
+++ b/solution.py
@@ -414,13 +414,6 @@
         slot_copy(k).start()
         return 0
 
-    lax.fori_loop(1, GROUPS, pack, 0)
-
-    ends.append(lambda: await_bytes(slots.at[pl.ds(0, GROUPS - 1)], slot_sem.at[0]))
-    one, two = blocks_for(me)
-    slots[me, 0] = masked(one)
-    slots[me, 1] = masked(two)
-
     def owner_copies(number, h, sends, lands):
         here = second[h][0]
         copies = []
@@ -470,10 +463,24 @@
     for h in range(2):
         term_out_1[h].finish()
         add_terms(h, term_out[h], sum_out[h], to_out[h])
+    for r in term_in_1:
+        r.forward()
+    lax.fori_loop(1, GROUPS, pack, 0)
+
+    ends.append(lambda: await_bytes(slots.at[pl.ds(0, GROUPS - 1)], slot_sem.at[0]))
+    one, two = blocks_for(me)
+    slots[me, 0] = masked(one)
+    slots[me, 1] = masked(two)
+
+    for h in range(2):
         for copy in out_own[h]:
             copy.start()
-    for r in term_in_1:
-        r.forward()
+
+    for h in range(2):
+        term_in_1[h].finish()
+        add_terms(h, term_in[h], sum_in[h], to_in[h])
+        for copy in in_own[h]:
+            copy.start()
 
     await_bytes(slots.at[pl.ds(0, GROUPS - 1)], slot_sem.at[1])
 
@@ -491,12 +498,6 @@
         return 0
 
     lax.fori_loop(0, 2 * GROUPS, apply_factor, 0, unroll=4)
-
-    for h in range(2):
-        term_in_1[h].finish()
-        add_terms(h, term_in[h], sum_in[h], to_in[h])
-        for copy in in_own[h]:
-            copy.start()
 
     def weigh(half, by):
         return [jnp.tile(by * w, (1, half // 128)) for w in weight]

time: 78.2 us -> 76.8 us (0.982)
  Pallas kernels: 77.5 us -> 76 us
    pallas_call x1, Pallas kernels: 74.2 us -> 72.7 us  [per_device(): pl.pallas_call(functools.partial(kernel, n_tensor), out_shape=(jax.ShapeD...]
where the time goes in v4:
time: 76.8 us; the launch traced here: 76.7 us
  Pallas kernels  76 us (99%)
    pallas_call x1, Pallas kernels, per_device(): pl.pallas_call(functools.partial(kernel, n_tensor), out_shape=(jax.ShapeD...  72.7 us
    pallas_call x1, Pallas kernels, per_device(): pl.pallas_call(place, out_shape=(jax.ShapeDtypeStruct((GROUPS * 2 * ROWS,...  3.3 us

profile of v4, /device:TPU:1, one launch (start us, length us, event | category | flops | bytes accessed | tf_op | source)
XLA Modules:
  0.0 76.7 jit_solution(3390017617000716466)
XLA Ops:
  0.6 72.7 %shard_map.111 = (bf16[4096,512]{1,0:T(8,128)(2,1)S(1)}, f32[4,16,512]{2,1,0:T(8,128)S(1)}, f32[4,16,1024]{2,1,0:T(8,128)S(1)}, f32[8,128]{1,0:T(8,128)S(1)}) custom-call(s32[256]{0:T(256)} %tenant_hbm.1, s32[256]{0:T(256)} %bitcast.1, s32[64]{0:T(128)} %tokens_hbm.1, s32[64]{0:T(128)} %owner_hbm.1, bf16[2048,512]{1,0:T(8,128)(2,1)} %x_hbm.1, ...), custom_call_target="tpu_custom_call" | custom-call | tf_op jit(solution)/shard_map/pallas_call | solution.py:612
  73.4 3.3 %shard_map.112 = (bf16[4096,512]{1,0:T(8,128)(2,1)}, f32[4,16,512]{2,1,0:T(8,128)}, f32[4,16,1024]{2,1,0:T(8,128)}, f32[4]{0:T(128)}) custom-call(bf16[4096,512]{1,0:T(8,128)(2,1)S(1)} %get-tuple-element.8.dg, f32[4,16,512]{2,1,0:T(8,128)S(1)} %get-tuple-element.9.gin, f32[4,16,1024]{2,1,0:T(8,128)S(1)} %get-tuple-element.10.gout, ...), custom_call_target="tpu_custom_call" | custom-call | tf_op jit(solution)/shard_map/pallas_call | solution.py:641

commit v5 on v4

--- a/solution.py
+++ b/solution.py
@@ -325,7 +325,7 @@
         )
 
     def over_tensor(do):
-        lax.fori_loop(1, n_tensor, lambda k, _: (do(k), 0)[1], 0)
+        lax.fori_loop(1, n_tensor, lambda k, _: (do(k), 0)[1], 0, unroll=5)
 
     def send_parts(part, got, number):
         over_tensor(lambda k: reduce_copy(part, got, number, k).start())
@@ -333,7 +333,7 @@
 
     def add_parts(part, got, full, number, scale):
         await_bytes(got.at[pl.ds(1, n_tensor - 1)], z_r.at[number])
-        total = lax.fori_loop(1, n_tensor, lambda k, acc: acc + got[k], part[pl.ds(t * bt, bt)])
+        total = lax.fori_loop(1, n_tensor, lambda k, acc: acc + got[k], part[pl.ds(t * bt, bt)], unroll=5)
         full[pl.ds(t * bt, bt)] = (scale * total).astype(BF16)
         over_tensor(lambda k: spread_copy(full, number + 1, k).start())
         ends.append(lambda: await_bytes(full.at[pl.ds(0, BLK - bt)], z_s.at[number + 1]))
@@ -531,7 +531,7 @@
     over_tensor(lambda k: square_copy(k).start())
     ends.append(lambda: await_bytes(sq_got.at[pl.ds(1, n_tensor - 1)], sq_sem.at[0]))
     await_bytes(sq_got.at[pl.ds(1, n_tensor - 1)], sq_sem.at[1])
-    total = lax.fori_loop(1, n_tensor, lambda k, acc: acc + sq_got[k], sq_own[...])
+    total = lax.fori_loop(1, n_tensor, lambda k, acc: acc + sq_got[k], sq_own[...], unroll=5)
     norm_ref[...] = jnp.sqrt(jnp.broadcast_to(jnp.sum(total, axis=1, keepdims=True), (8, 128)))
 
     for end in ends:

time: 76.8 us -> 76.8 us (level)
  no operation moved by 1% of the time
where the time goes in v5:
time: 76.8 us; the launch traced here: 76.5 us
  Pallas kernels  75.9 us (99%)
    pallas_call x1, Pallas kernels, per_device(): pl.pallas_call(functools.partial(kernel, n_tensor), out_shape=(jax.ShapeD...  72.5 us
    pallas_call x1, Pallas kernels, per_device(): pl.pallas_call(place, out_shape=(jax.ShapeDtypeStruct((GROUPS * 2 * ROWS,...  3.3 us

profile of v5, /device:TPU:1, one launch (start us, length us, event | category | flops | bytes accessed | tf_op | source)
XLA Modules:
  0.0 76.5 jit_solution(18128710481694934366)
XLA Ops:
  0.6 72.5 %shard_map.111 = (bf16[4096,512]{1,0:T(8,128)(2,1)S(1)}, f32[4,16,512]{2,1,0:T(8,128)S(1)}, f32[4,16,1024]{2,1,0:T(8,128)S(1)}, f32[8,128]{1,0:T(8,128)S(1)}) custom-call(s32[256]{0:T(256)} %tenant_hbm.1, s32[256]{0:T(256)} %bitcast.1, s32[64]{0:T(128)} %tokens_hbm.1, s32[64]{0:T(128)} %owner_hbm.1, bf16[2048,512]{1,0:T(8,128)(2,1)} %x_hbm.1, ...), custom_call_target="tpu_custom_call" | custom-call | tf_op jit(solution)/shard_map/pallas_call | solution.py:612
  73.2 3.3 %shard_map.112 = (bf16[4096,512]{1,0:T(8,128)(2,1)}, f32[4,16,512]{2,1,0:T(8,128)}, f32[4,16,1024]{2,1,0:T(8,128)}, f32[4]{0:T(128)}) custom-call(bf16[4096,512]{1,0:T(8,128)(2,1)S(1)} %get-tuple-element.8.dg, f32[4,16,512]{2,1,0:T(8,128)S(1)} %get-tuple-element.9.gin, f32[4,16,1024]{2,1,0:T(8,128)S(1)} %get-tuple-element.10.gout, ...), custom_call_target="tpu_custom_call" | custom-call | tf_op jit(solution)/shard_map/pallas_call | solution.py:641
